TPU v7x, 512 devices: a whole 4x8x8 slice. The times are simulated.
512 devices in a mesh: rep: 16 (over z_hi, y), shard: 32 (over z_lo, x, core).
Axes of the slice: x: 4, y: 8, z: 8 (z_hi: 2, z_lo: 4; z = z_hi * 4 + z_lo), core: 2. Of those that a mesh axis runs over, the one named last changes fastest.
Arguments:
- activations: bfloat16 [65536, 8192], P('rep', 'shard'), may hold values from -6 to 6
- key_grads: bfloat16 [65536, 1024], P(('rep', 'shard')), may hold values from -0.09375 to 0.09375
- momentum: float32 [131072, 1024], P(('rep', 'shard')), may hold values from -6 to 6
- freq_rows: int32 [128, 16, 8], replicated, may hold values from 0 to 15, as said below
- freq_cols: int32 [128, 16, 8], replicated, may hold values from 0 to 15, as said below
- dispatch: int32 [32, 64], replicated, may hold values from 0 to 63, each once within a row
Outputs:
- new_momentum: float32 [131072, 1024], P(('rep', 'shard'))
- update: bfloat16 [2048, 4096], P('shard')
Inputs may be any that keep to these rules, and one draw needn't show every extreme that they name: `freq_rows`: the 8 entries of one span are distinct. `freq_cols`: the 8 entries of one span are distinct. `dispatch`: each row names every number below 64 once.
All inputs are finite; a program needn't handle non-finite values.
Results may differ from a plain program's by a relative error of at most 0.001.
Values may be sent and summed in bfloat16 or wider, within the bound.
No kernel may reach another device: no remote copies, remote signals or barrier semaphores. Data moves between devices by JAX's collectives and lax.ppermute only.
A program may use at most 64 MiB of HBM per device.

v0:
```python
import jax
import jax.numpy as jnp
from jax import lax
from jax.sharding import PartitionSpec as P

CH = 64
K = 8


def dct_table(size, dtype):
    frequency = jnp.arange(size, dtype=jnp.int32).astype(dtype)[:, None]
    sample = jnp.arange(size, dtype=jnp.int32).astype(dtype)[None, :]
    scales = jnp.where(frequency == 0, jnp.sqrt(1.0 / size), jnp.sqrt(2.0 / size)).astype(dtype)
    return scales * jnp.cos(jnp.pi * (2.0 * sample + 1.0) * frequency / (2.0 * size))


def basis_rows(indices, table):
    onehot = (indices[..., None] == jnp.arange(table.shape[0], dtype=jnp.int32)).astype(table.dtype)
    return jnp.einsum("...kf,fn->...kn", onehot, table, precision=lax.Precision.HIGHEST)


def encode(blocks, row_basis, col_basis):
    partial_rows = jnp.einsum("abin,anbm->abim", row_basis, blocks, precision=lax.Precision.HIGHEST)
    return jnp.einsum("abim,abjm->abij", partial_rows, col_basis, precision=lax.Precision.HIGHEST)


def body(activations, key_grads, momentum, freq_rows, freq_cols, dispatch):
    shards = lax.axis_size("shard")
    position = lax.axis_index("shard")
    local_rows = momentum.shape[0]
    width = momentum.shape[1]
    side = CH
    kept = K
    row_blocks = local_rows // side
    col_count = width // side
    per_spans = row_blocks * col_count
    per_owner = per_spans // shards
    table = dct_table(side, jnp.float32)
    grad = lax.dot_general(
        activations,
        lax.all_gather(key_grads, "shard", axis=0, tiled=True),
        (((0,), (0,)), ((), ())),
        preferred_element_type=jnp.float32,
    )
    fresh = 0.999 * momentum + grad
    my_rows = lax.dynamic_slice_in_dim(freq_rows, position * row_blocks, row_blocks, 0)
    my_cols = lax.dynamic_slice_in_dim(freq_cols, position * row_blocks, row_blocks, 0)
    row_basis = basis_rows(my_rows, table)
    col_basis = basis_rows(my_cols, table)
    blocks = fresh.reshape(row_blocks, side, col_count, side)
    corner = encode(blocks, row_basis, col_basis)
    partial_rows = jnp.einsum("abij,abin->abnj", corner, row_basis, precision=lax.Precision.HIGHEST)
    local = jnp.einsum("abnj,abjm->anbm", partial_rows, col_basis, precision=lax.Precision.HIGHEST)
    new_momentum = fresh - local.reshape(local_rows, width)
    flat_corner = corner.reshape(per_spans, kept * kept)
    own_slots = lax.dynamic_slice_in_dim(dispatch, position * per_owner, per_owner, 1)
    span_ids = (jnp.arange(shards, dtype=jnp.int32)[:, None] * per_spans + own_slots).reshape(-1)
    board = jnp.zeros((shards, per_spans * kept * kept), jnp.float32)
    board = lax.dynamic_update_slice(
        board, flat_corner.reshape(1, per_spans * kept * kept), (position, 0)
    )
    summed = lax.psum(board, ("rep", "shard"))
    owned = summed.reshape(shards * per_spans, kept * kept)[span_ids]
    owned = owned.reshape(shards * per_owner, kept, kept)
    owned_rows = basis_rows(freq_rows.reshape(-1, kept)[span_ids], table)
    owned_cols = basis_rows(freq_cols.reshape(-1, kept)[span_ids], table)
    decoded = jnp.einsum("cij,cin->cnj", owned, owned_rows, precision=lax.Precision.HIGHEST)
    decoded = jnp.einsum("cnj,cjm->cnm", decoded, owned_cols, precision=lax.Precision.HIGHEST)
    update = decoded.reshape(shards * per_owner, side * side).astype(jnp.bfloat16)
    return (new_momentum, update)


def solution(mesh):
    in_specs = (
        P("rep", "shard"),
        P(("rep", "shard"), None),
        P(("rep", "shard"), None),
        P(),
        P(),
        P(),
    )
    out_specs = (P(("rep", "shard"), None), P("shard", None))
    return jax.shard_map(body, mesh=mesh, in_specs=in_specs, out_specs=out_specs, check_vma=False)
```

profile of v0, /device:TPU:1, one launch (start us, length us, event | category | flops | bytes accessed | tf_op | source)
XLA Modules:
  0.0 395.5 jit_solution(12604512850149879888)
XLA Ops:
  8.0 2.2 copy.20
  10.2 1.3 copy.22
  12.1 1.8 gather_fusion
  15.0 1.1 fusion.5
  16.6 1.2 fusion.8
  17.8 1.2 fusion.6
  19.0 69.4 %all-gather.2.cloned.1.call-done = bf16[4096,1024]{1,0:T(8,128)(2,1)} async-done(((bf16[128,1024]{1,0:T(8,128)(2,1)}), bf16[4096,1024]{1,0:T(8,128)(2,1)}) %all-gather.2.cloned.1.call-update) | async-done | bytes 8388624 | tf_op jit(solution)/shard_map/all_gather | solution.py:41
  88.4 6.0 %convolution_add_fusion = f32[256,1024]{1,0:T(8,128)S(1)} fusion(bf16[4096,256]{1,0:T(8,128)(2,1)S(1)} %copy-done, bf16[4096,1024]{1,0:T(8,128)(2,1)} %all-gather.2.cloned.1.call-done, f32[256,1024]{1,0:T(8,128)} %param.8), kind=kOutput, calls=%fused_computation.7 | convolution fusion | flops 2148007936 | bytes 12582912 | tf_op jit(solution)/shard_map/dot_general | solution.py:39
  94.3 1.9 reshape.84
  96.2 4.0 %fusion = f32[4,16,8,64]{3,2,1,0:T(8,128)S(1)} fusion(f32[4,64,16,64]{3,2,1,0:T(8,128)} %reshape.84, f32[4,16,8,64]{3,1,2,0:T(8,128)} %fusion.5), kind=kOutput, calls=%fused_computation.3 | convolution fusion | flops 25165824 | bytes 1310720 | tf_op jit(solution)/shard_map/abin,anbm->abim/dot_general | solution.py:23
  101.5 1.4 fusion.12
  102.9 1.1 reshape_reshape.3
  104.0 0.8 broadcast_in_dim.12
  104.9 1.6 dynamic_update_slice.3
  106.5 2.5 reshape.88
  109.0 5.9 %convolution_bitcast_fusion = f32[4,64,16,64]{1,3,2,0:T(8,128)} fusion(f32[4,16,8,64]{3,2,1,0:T(8,128)S(1)} %fusion.10, f32[4,16,64,8]{2,3,1,0:T(8,128)} %fusion.12), kind=kOutput, calls=%fused_computation.5 | convolution fusion | flops 25165824 | bytes 1310720 | tf_op jit(solution)/shard_map/abnj,abjm->anbm/dot_general | solution.py:53
  114.9 3.1 copy.19
  118.0 2.7 reshape.85
  120.7 2.4 sub.3
  123.1 256.7 %all-reduce.2.cloned.1.call-done = f32[2048,64]{1,0:T(8,128)} async-done(((f32[2048,64]{1,0:T(8,128)}), f32[2048,64]{1,0:T(8,128)}) %all-reduce.2.cloned.1.call-update) | async-done | bytes 524304 | tf_op jit(solution)/shard_map/psum | solution.py:62
  379.8 1.8 gather_fusion.1
  381.9 0.8 fusion.3
  382.6 4.4 %convolution_convert_fusion = bf16[64,64,64]{2,1,0:T(8,128)(2,1)S(1)} fusion(f32[64,64,8]{1,2,0:T(8,128)S(1)} %fusion.3, f32[64,8,64]{2,0,1:T(8,128)} %fusion.6), kind=kOutput, calls=%fused_computation.6 | convolution fusion | flops 25427968 | bytes 786432 | tf_op jit(solution)/shard_map/cnj,cjm->cnm/dot_general | solution.py:68
  387.0 1.6 convert_element_type.33
  (36 shorter events, 4.3 us)
Async XLA Ops:
  7.2 81.2 %copy-start = (bf16[4096,256]{1,0:T(8,128)(2,1)S(1)}, bf16[4096,256]{1,0:T(8,128)(2,1)}, u32[]{:S(2)}) copy-start(bf16[4096,256]{1,0:T(8,128)(2,1)} %param.6) | copy-start | bytes 6291460
  7.2 4.3 %copy-start.4 = (s32[128,16,8]{0,2,1:T(8,128)S(1)}, s32[128,16,8]{0,2,1:T(8,128)}, u32[]{:S(2)}) copy-start(s32[128,16,8]{0,2,1:T(8,128)} %param.9) | copy-start | bytes 196612
  7.2 4.3 %copy-start.5 = (s32[128,16,8]{0,2,1:T(8,128)S(1)}, s32[128,16,8]{0,2,1:T(8,128)}, u32[]{:S(2)}) copy-start(s32[128,16,8]{0,2,1:T(8,128)} %param.10) | copy-start | bytes 196612
  7.2 4.7 %copy-start.6 = (s32[32,64]{1,0:T(8,128)S(1)}, s32[32,64]{1,0:T(8,128)}, u32[]{:S(2)}) copy-start(s32[32,64]{1,0:T(8,128)} %param.11) | copy-start | bytes 24580
  7.2 81.1 %all-gather.2.cloned.1.call-start = ((), (), s32[]{:S(2)}) async-start(), calls=%async_computation | async-start | bytes 8650752 | tf_op jit(solution)/shard_map/all_gather | solution.py:41
  7.9 371.8 %all-reduce.2.cloned.1.call-start = ((), (), s32[]{:S(2)}) async-start(), calls=%async_computation.1 | async-start | bytes 2097152 | tf_op jit(solution)/shard_map/psum | solution.py:62
  96.2 5.3 %copy-start.2 = (f32[4,16,8,64]{3,1,2,0:T(8,128)S(1)}, f32[4,16,8,64]{3,1,2,0:T(8,128)}, u32[]{:S(2)}) copy-start(f32[4,16,8,64]{3,1,2,0:T(8,128)} %fusion.5) | copy-start | bytes 393220
  100.8 0.7 copy-start.1
  120.7 261.2 %copy-start.3 = (f32[64,8,64]{2,0,1:T(8,128)S(1)}, f32[64,8,64]{2,0,1:T(8,128)}, u32[]{:S(2)}) copy-start(f32[64,8,64]{2,0,1:T(8,128)} %fusion.8) | copy-start | bytes 393220
Sparse Core Ops, SparseCore 0:
  10.2 78.1 all-gather.1
  109.1 270.6 all-reduce.1
where the time goes:
time: 396 us; the launch traced here: 395 us
  waiting for transfers between devices  327 us (83%)
  matrix products  27 us (7%)
  local copies, waits for them, and re-layouts  24.5 us (6%)
  between operations  14.2 us (4%)
    psum x1, waiting for transfers between devices, body(): summed = lax.psum(board, ('rep', 'shard'))  257 us
    all_gather x1, waiting for transfers between devices, body(): lax.all_gather(key_grads, 'shard', axis=0, tiled=True)  69.4 us
  transfers between devices with their start and end apart: 2, of which 2 were waited for; matrix products, arithmetic and copies ran while one was open for 6% of the time, Pallas kernels for 0%

commit v1 on v0

v1 whole, which is shorter than its diff:
```python
import functools

import jax
import jax.numpy as jnp
import numpy as np
from jax import lax
from jax.experimental import pallas as pl
from jax.experimental.pallas import tpu as pltpu
from jax.sharding import PartitionSpec as P

CH = 64
K = 8
BAND = 16
ROWS = 256
WIDTH = 1024
F32 = jnp.float32
BF16 = jnp.bfloat16


def band_table():
    frequency = np.arange(BAND)[:, None]
    sample = np.arange(CH)[None, :]
    scales = np.where(frequency == 0, np.sqrt(1.0 / CH), np.sqrt(2.0 / CH))
    return scales * np.cos(np.pi * (2.0 * sample + 1.0) * frequency / (2.0 * CH))


def split_np(x):
    hi = x.astype(np.float32).astype(jnp.bfloat16)
    lo = (x - hi.astype(np.float64)).astype(np.float32).astype(jnp.bfloat16)
    return hi, lo


def block_basis():
    return np.kron(np.eye(4), band_table())


def pair_basis():
    return np.kron(band_table(), band_table())


def split(x):
    hi = x.astype(BF16)
    return hi, (x - hi.astype(F32)).astype(BF16)


def dot(x, y):
    return lax.dot_general(x, y, (((1,), (0,)), ((), ())), preferred_element_type=F32)


def dot3(x, y):
    (xh, xl), (yh, yl) = x, y
    return dot(xh, yh) + (dot(xh, yl) + dot(xl, yh))


def lanes(x, index):
    return jnp.take_along_axis(x, index, axis=1)


def encode_kernel(fresh, lh, ll, th, tl, mask, col_index, row_pick, slot_row, slot_lane, new, sent):
    left, right = (lh[...], ll[...]), (th[...], tl[...])
    whole = fresh[...]
    half = dot3(left, split(whole))
    parts = [dot3(split(half[:, q * 256:(q + 1) * 256]), right) for q in range(4)]
    low = jnp.concatenate(parts[:2], axis=1)
    high = jnp.concatenate(parts[2:], axis=1)

    lane = lax.broadcasted_iota(jnp.int32, (BAND, 128), 1)
    picked = []
    for a in range(4):
        rows = slice(a * BAND, (a + 1) * BAND)
        index = jnp.broadcast_to(col_index[a:a + 1, :], (BAND, 128))
        cols = jnp.where(lane < 64, lanes(low[rows], index), lanes(high[rows], index))
        want = row_pick[a * K:(a + 1) * K, :]
        total = jnp.zeros((K, 128), F32)
        for f in range(BAND):
            total = jnp.where(want == f, jnp.broadcast_to(cols[f:f + 1], (K, 128)), total)
        picked.append(total)
    code, place = slot_row[...], slot_lane[...]
    board = jnp.zeros((32, 128), F32)
    for a in range(4):
        for i in range(K):
            row = jnp.broadcast_to(picked[a][i:i + 1], (32, 128))
            board = jnp.where(code == a * K + i, lanes(row, place), board)
    sent[...] = board

    kept = [low * mask[:, :128], high * mask[:, 128:]]
    back = [dot3(right, split(part)) for part in kept]
    for q in range(4):
        piece = back[q // 2][:, (q % 2) * 64:(q % 2) * 64 + 64]
        cols = slice(q * 256, (q + 1) * 256)
        new[:, cols] = whole[:, cols] - dot3(split(piece), left)


def decode_kernel(received, index, kh, kl, out, first, second):
    total = received[0:32, :]
    for r in range(1, 16):
        total = total + received[r * 32:(r + 1) * 32, :]
    for k in range(2):
        for h in range(2):
            where = index[k * 32:(k + 1) * 32, h * 128:(h + 1) * 128]
            value = lanes(total, jnp.maximum(where, 0))
            spread = (first, second)[h]
            spread[pl.ds(k, 32, stride=2), :] = jnp.where(where >= 0, value, 0.0)
    pair = split(jnp.concatenate([first[...], second[...]], axis=1))
    for n in range(8):
        cols = slice(n * 512, (n + 1) * 512)
        out[:, cols] = dot3(pair, (kh[:, cols], kl[:, cols])).astype(BF16)


def vmem(n):
    return [pl.BlockSpec(memory_space=pltpu.VMEM)] * n


def encode(fresh, tables):
    lh, ll = split_np(block_basis())
    return pl.pallas_call(
        encode_kernel,
        out_shape=(jax.ShapeDtypeStruct((ROWS, WIDTH), F32), jax.ShapeDtypeStruct((32, 128), F32)),
        in_specs=vmem(10),
        out_specs=tuple(vmem(2)),
        compiler_params=pltpu.CompilerParams(vmem_limit_bytes=40 << 20),
        name="encode",
    )(fresh, lh, ll, lh.T.copy(), ll.T.copy(), *tables)


def decode(received, index):
    kh, kl = split_np(pair_basis())
    return pl.pallas_call(
        decode_kernel,
        out_shape=jax.ShapeDtypeStruct((64, CH * CH), BF16),
        in_specs=vmem(4),
        out_specs=pl.BlockSpec(memory_space=pltpu.VMEM),
        scratch_shapes=[pltpu.VMEM((64, 128), F32)] * 2,
        compiler_params=pltpu.CompilerParams(vmem_limit_bytes=40 << 20),
        name="decode",
    )(received, index, kh, kl)


def sender_tables(my_rows, my_cols, slots):
    band = jnp.arange(BAND, dtype=jnp.int32)
    in_rows = jnp.any(my_rows[..., None] == band, axis=2)
    in_cols = jnp.any(my_cols[..., None] == band, axis=2)
    mask = jnp.transpose(in_rows, (0, 2, 1))[..., None] & in_cols[:, None]
    mask = mask.reshape(4 * BAND, 16 * BAND).astype(F32)
    offset = (jnp.arange(16, dtype=jnp.int32) % 8 * BAND)[None, :, None]
    col_index = (my_cols + offset).reshape(4, 128)
    row_pick = jnp.broadcast_to(jnp.transpose(my_rows, (0, 2, 1))[..., None], (4, K, 16, K)).reshape(32, 128)
    order = slots.reshape(32, 2, 1, 1)
    i = jnp.arange(K, dtype=jnp.int32)
    slot_row = jnp.broadcast_to(order // 16 * K + i[:, None], (32, 2, K, K)).reshape(32, 128)
    slot_lane = jnp.broadcast_to(order % 16 * K + i, (32, 2, K, K)).reshape(32, 128)
    return mask, col_index, row_pick, slot_row, slot_lane


def owner_table(rows, cols):
    band = jnp.arange(BAND, dtype=jnp.int32)
    i = jnp.arange(K, dtype=jnp.int32)[:, None]

    def places(freq):
        hit = freq[..., None] == band
        return jnp.any(hit, axis=2), jnp.sum(jnp.where(hit, i, 0), axis=2)

    (row_in, row_at), (col_in, col_at) = places(rows), places(cols)
    start = (jnp.arange(2, dtype=jnp.int32) * 64)[None, :, None, None]
    index = start + row_at[..., None] * K + col_at[:, :, None]
    index = jnp.where(row_in[..., None] & col_in[:, :, None], index, -1)
    return jnp.transpose(index, (1, 0, 2, 3)).reshape(64, BAND * BAND)


def body(activations, key_grads, momentum, freq_rows, freq_cols, dispatch):
    position = lax.axis_index("shard")
    grad = lax.dot_general(
        activations,
        lax.all_gather(key_grads, "shard", axis=0, tiled=True),
        (((0,), (0,)), ((), ())),
        preferred_element_type=F32,
    )
    fresh = 0.999 * momentum + grad
    my_rows = lax.dynamic_slice_in_dim(freq_rows, position * 4, 4, 0)
    my_cols = lax.dynamic_slice_in_dim(freq_cols, position * 4, 4, 0)
    slots = lax.dynamic_slice_in_dim(dispatch, position, 1, 0).reshape(64)
    new_momentum, board = encode(fresh, sender_tables(my_rows, my_cols, slots))

    own = lax.dynamic_slice_in_dim(dispatch, position * 2, 2, 1)
    span_ids = (jnp.arange(32, dtype=jnp.int32)[:, None] * 64 + own).reshape(-1)
    own_rows = freq_rows.reshape(-1, K)[span_ids].reshape(32, 2, K)
    own_cols = freq_cols.reshape(-1, K)[span_ids].reshape(32, 2, K)
    index = owner_table(own_rows, own_cols)
    board = jnp.broadcast_to(board[None], (16, 32, 128)).reshape(512, 128)
    received = lax.all_to_all(board, ("rep", "shard"), 0, 0, tiled=True)
    update = decode(received, index)
    return (new_momentum, update)


def solution(mesh):
    in_specs = (
        P("rep", "shard"),
        P(("rep", "shard"), None),
        P(("rep", "shard"), None),
        P(),
        P(),
        P(),
    )
    out_specs = (P(("rep", "shard"), None), P("shard", None))
    return jax.shard_map(body, mesh=mesh, in_specs=in_specs, out_specs=out_specs, check_vma=False)
```

time: 396 us -> 141 us (0.36)
  waiting for transfers between devices: 327 us -> 85.2 us
  matrix products: 27 us -> 5.73 us
  starting transfers between devices: 0.08 us -> 14.8 us
  local copies, waits for them, and re-layouts: 24.5 us -> 15.4 us
  Pallas kernels: 0 us -> 4.5 us
    psum x1 -> x0, waiting for transfers between devices: 257 us -> none  [body(): summed = lax.psum(board, ('rep', 'shard'))]
    dot_general x10 -> x0, matrix products: 21 us -> none  [the longest x1 5.9 us: body(): jnp.einsum('abnj,abjm->anbm', partial_rows, col_basis, precision=lax.Prec...]
    all_to_all x0 -> x1, waiting for transfers between devices: none -> 16.3 us  [body(): received = lax.all_to_all(board, ('rep', 'shard'), 0, 0, tiled=True)]
    all_to_all x0 -> x1, starting transfers between devices: none -> 14.8 us  [body(): received = lax.all_to_all(board, ('rep', 'shard'), 0, 0, tiled=True)]
    reshape x5, local copies, waits for them, and re-layouts: 7.35 us -> 0.47 us  [the longest x1 0.15 us: sender_tables(): jnp.broadcast_to(jnp.transpose(my_rows, (0, 2, 1))[..., None], (4, K, 16,...]
    pallas_call x0 -> x2, Pallas kernels: none -> 4.5 us  [the longest x1 2.42 us: encode(): pl.pallas_call(encode_kernel, out_shape=(jax.ShapeDtypeStruct((ROWS, WIDT...]
  transfers between devices with their start and end apart: 2 -> 2, of which waited for: 2 -> 2; matrix products, arithmetic and copies ran while one was open for 6% -> 9% of each run, Pallas kernels for 0% -> 0%
where the time goes in v1:
time: 141 us
  waiting for transfers between devices  85.2 us (60%)
  local copies, waits for them, and re-layouts  15.4 us (11%)
  starting transfers between devices  14.8 us (10%)
  between operations  14.3 us (10%)
  matrix products  5.73 us (4%)
  Pallas kernels  4.5 us (3%)
    all_gather x1, waiting for transfers between devices, body(): lax.all_gather(key_grads, 'shard', axis=0, tiled=True)  68.2 us
    all_to_all x1, waiting for transfers between devices, body(): received = lax.all_to_all(board, ('rep', 'shard'), 0, 0, tiled=True)  16.3 us
    all_to_all x1, starting transfers between devices, body(): received = lax.all_to_all(board, ('rep', 'shard'), 0, 0, tiled=True)  14.8 us
    unnamed x21, local copies, waits for them, and re-layouts  7.89 us
    dot_general x1, matrix products, body(): lax.dot_general(activations, lax.all_gather(key_grads, 'shard', axis=0, t...  5.73 us
  transfers between devices with their start and end apart: 2, of which 2 were waited for; matrix products, arithmetic and copies ran while one was open for 9% of the time, Pallas kernels for 0%

profile of v1, /device:TPU:1, one launch (start us, length us, event | category | flops | bytes accessed | tf_op | source)
XLA Modules:
  0.0 141.0 jit_solution(7311550773472903735)
XLA Ops:
  7.2 0.7 all-gather.2.cloned.1.call-update
  7.9 1.0 constant_dynamic-slice_fusion.1
  8.9 0.2 copy.63
  9.2 2.2 %copy.75 = s32[128,16,8]{2,1,0:T(8,128)} copy(s32[128,16,8]{0,2,1:T(8,128)} %param.16) | data formatting | bytes 131072 | tf_op args[4]
  11.4 2.3 %copy.72 = s32[128,16,8]{2,1,0:T(8,128)} copy(s32[128,16,8]{0,2,1:T(8,128)} %param.15) | data formatting | bytes 131072 | tf_op args[3]
  13.7 0.2 copy.60
  13.9 0.2 fusion
  14.2 0.2 fusion.1
  14.3 0.2 and_convert_fusion
  14.5 0.2 reshape.222.mask
  15.3 0.2 reshape.216.row_pick
  16.1 1.8 %gather_fusion.1 = s32[64,8]{1,0:T(8,128)S(1)} fusion(s32[2048,8]{1,0:T(8,128)} %bitcast.27, s32[1024]{0:T(1024)S(1)} %pad_clamp_fusion), kind=kCustom, calls=%fused_computation.1 | custom fusion | bytes 4352 | tf_op jit(solution)/shard_map/gather | solution.py:187
  18.0 1.8 %gather_fusion = s32[64,8]{1,0:T(8,128)S(1)} fusion(s32[2048,8]{1,0:T(8,128)} %bitcast.26, s32[1024]{0:T(1024)S(1)} %pad_clamp_fusion), kind=kCustom, calls=%fused_computation | custom fusion | bytes 4352 | tf_op jit(solution)/shard_map/gather | solution.py:186
  20.1 68.2 %all-gather.2.cloned.1.call-done = bf16[4096,1024]{1,0:T(8,128)(2,1)} async-done(((bf16[128,1024]{1,0:T(8,128)(2,1)}), bf16[4096,1024]{1,0:T(8,128)(2,1)}) %all-gather.2.cloned.1.call-update) | async-done | bytes 8388624 | tf_op jit(solution)/shard_map/all_gather | solution.py:174
  88.3 5.7 %convolution_add_fusion.fresh = f32[256,1024]{1,0:T(8,128)S(1)} fusion(bf16[4096,256]{1,0:T(8,128)(2,1)S(1)} %copy-done, bf16[4096,1024]{1,0:T(8,128)(2,1)} %all-gather.2.cloned.1.call-done, f32[256,1024]{1,0:T(8,128)S(1)} %copy-done.7), kind=kOutput, calls=%fused_computation.2 | convolution fusion | flops 2148007936 | bytes 12582912 | tf_op jit(solution)/shard_map/dot_general | solution.py:172
  94.1 2.4 %encode.1 = (f32[256,1024]{1,0:T(8,128)}, f32[32,128]{1,0:T(8,128)S(1)}) custom-call(f32[256,1024]{1,0:T(8,128)S(1)} %convolution_add_fusion.fresh, bf16[64,256]{1,0:T(8,128)(2,1)S(1)} %copy-done.5, bf16[64,256]{1,0:T(8,128)(2,1)S(1)} %copy-done.6, bf16[256,64]{1,0:T(8,128)(2,1)S(1)} %copy-done.3, bf16[256,64]{1,0:T(8,128)(2,1)S(1)} %copy-done.4, ...), custom_call_target="tpu_custom_call" | custom-call | tf_op jit(solution)/shard_map/encode/pallas_call | solution.py:116
  96.5 0.7 broadcast_in_dim.32
  97.3 14.8 %all-to-all-start = ((f32[512,1,128]{2,1,0:T(1,128)}), f32[512,1,128]{2,1,0:T(1,128)S(1)}, u32[]{:S(2)}, u32[]{:S(2)}) async-start(f32[512,1,128]{2,1,0:T(1,128)} %bitcast.4), calls=%async_computation | async-start | bytes 524288 | tf_op jit(solution)/shard_map/all_to_all | solution.py:190
  112.1 0.2 and_select_fusion
  112.3 0.2 select_n.79
  112.6 16.3 %all-to-all-done = f32[512,1,128]{2,1,0:T(1,128)S(1)} async-done(((f32[512,1,128]{2,1,0:T(1,128)}), f32[512,1,128]{2,1,0:T(1,128)S(1)}, u32[]{:S(2)}, u32[]{:S(2)}) %all-to-all-start) | async-done | bytes 262176 | tf_op jit(solution)/shard_map/all_to_all | solution.py:190
  128.9 1.6 %copy-done.1 = bf16[256,4096]{1,0:T(8,128)(2,1)S(1)} copy-done((bf16[256,4096]{1,0:T(8,128)(2,1)S(1)}, bf16[256,4096]{1,0:T(8,128)(2,1)}, u32[]{:S(2)}) %copy-start.1) | copy-done | bytes 2097176
  130.5 1.6 %copy-done.2 = bf16[256,4096]{1,0:T(8,128)(2,1)S(1)} copy-done((bf16[256,4096]{1,0:T(8,128)(2,1)S(1)}, bf16[256,4096]{1,0:T(8,128)(2,1)}, u32[]{:S(2)}) %copy-start.2) | copy-done | bytes 2097176
  132.1 2.1 %decode.1 = bf16[64,4096]{1,0:T(8,128)(2,1)} custom-call(f32[512,128]{1,0:T(8,128)S(1)} %bitcast.25, s32[64,256]{1,0:T(8,128)S(1)} %copy.80.index, bf16[256,4096]{1,0:T(8,128)(2,1)S(1)} %copy-done.1, bf16[256,4096]{1,0:T(8,128)(2,1)S(1)} %copy-done.2), custom_call_target="tpu_custom_call" | custom-call | tf_op jit(solution)/shard_map/decode/pallas_call | solution.py:128
  (52 shorter events, 1.8 us)
Async XLA Ops:
  7.2 81.2 %copy-start = (bf16[4096,256]{1,0:T(8,128)(2,1)S(1)}, bf16[4096,256]{1,0:T(8,128)(2,1)}, u32[]{:S(2)}) copy-start(bf16[4096,256]{1,0:T(8,128)(2,1)} %param.12) | copy-start | bytes 6291460
  7.2 81.1 %all-gather.2.cloned.1.call-start = ((), (), s32[]{:S(2)}) async-start(), calls=%async_computation.1 | async-start | bytes 8650752 | tf_op jit(solution)/shard_map/all_gather | solution.py:174
  9.2 6.2 %copy-start.8 = (s32[32,64]{1,0:T(8,128)S(1)}, s32[32,64]{1,0:T(8,128)}, u32[]{:S(2)}) copy-start(s32[32,64]{1,0:T(8,128)} %param.17) | copy-start | bytes 24580
  14.8 73.5 %copy-start.7 = (f32[256,1024]{1,0:T(8,128)S(1)}, f32[256,1024]{1,0:T(8,128)}, u32[]{:S(2)}) copy-start(f32[256,1024]{1,0:T(8,128)} %param.14) | copy-start | bytes 3145732
  20.0 74.0 %copy-start.3 = (bf16[256,64]{1,0:T(8,128)(2,1)S(1)}, bf16[256,64]{1,0:T(8,128)(2,1)}, u32[]{:S(2)}) copy-start(bf16[256,64]{1,0:T(8,128)(2,1)} %constant.84.clone.th) | copy-start | bytes 98308
  20.0 74.0 %copy-start.4 = (bf16[256,64]{1,0:T(8,128)(2,1)S(1)}, bf16[256,64]{1,0:T(8,128)(2,1)}, u32[]{:S(2)}) copy-start(bf16[256,64]{1,0:T(8,128)(2,1)} %constant.85.clone.tl) | copy-start | bytes 98308
  20.1 74.0 %copy-start.5 = (bf16[64,256]{1,0:T(8,128)(2,1)S(1)}, bf16[64,256]{1,0:T(8,128)(2,1)}, u32[]{:S(2)}) copy-start(bf16[64,256]{1,0:T(8,128)(2,1)} %constant.82.clone.lh) | copy-start | bytes 98308
  20.1 74.0 %copy-start.6 = (bf16[64,256]{1,0:T(8,128)(2,1)S(1)}, bf16[64,256]{1,0:T(8,128)(2,1)}, u32[]{:S(2)}) copy-start(bf16[64,256]{1,0:T(8,128)(2,1)} %constant.83.clone.ll) | copy-start | bytes 98308
  97.3 31.6 %all-to-all-start = ((f32[512,1,128]{2,1,0:T(1,128)}), f32[512,1,128]{2,1,0:T(1,128)S(1)}, u32[]{:S(2)}, u32[]{:S(2)}) async-start(f32[512,1,128]{2,1,0:T(1,128)} %bitcast.4), calls=%async_computation | async-start | bytes 524288 | tf_op jit(solution)/shard_map/all_to_all | solution.py:190
  128.9 1.6 %copy-start.1 = (bf16[256,4096]{1,0:T(8,128)(2,1)S(1)}, bf16[256,4096]{1,0:T(8,128)(2,1)}, u32[]{:S(2)}) copy-start(bf16[256,4096]{1,0:T(8,128)(2,1)} %constant.86.clone.kh) | copy-start | bytes 6291460
  130.5 1.6 %copy-start.2 = (bf16[256,4096]{1,0:T(8,128)(2,1)S(1)}, bf16[256,4096]{1,0:T(8,128)(2,1)}, u32[]{:S(2)}) copy-start(bf16[256,4096]{1,0:T(8,128)(2,1)} %constant.87.clone.kl) | copy-start | bytes 6291460
Sparse Core Ops, SparseCore 0:
  10.2 78.1 all-gather.1

commit v2 on v1

--- a/solution.py
+++ b/solution.py
@@ -13,6 +13,7 @@
 BAND = 16
 ROWS = 256
 WIDTH = 1024
+SCALE = 2.0 ** 15
 F32 = jnp.float32
 BF16 = jnp.bfloat16
 
@@ -56,14 +57,7 @@
     return jnp.take_along_axis(x, index, axis=1)
 
 
-def encode_kernel(fresh, lh, ll, th, tl, mask, col_index, row_pick, slot_row, slot_lane, new, sent):
-    left, right = (lh[...], ll[...]), (th[...], tl[...])
-    whole = fresh[...]
-    half = dot3(left, split(whole))
-    parts = [dot3(split(half[:, q * 256:(q + 1) * 256]), right) for q in range(4)]
-    low = jnp.concatenate(parts[:2], axis=1)
-    high = jnp.concatenate(parts[2:], axis=1)
-
+def select(low, high, col_index, row_pick, slot_row, slot_lane):
     lane = lax.broadcasted_iota(jnp.int32, (BAND, 128), 1)
     picked = []
     for a in range(4):
@@ -81,14 +75,78 @@
         for i in range(K):
             row = jnp.broadcast_to(picked[a][i:i + 1], (32, 128))
             board = jnp.where(code == a * K + i, lanes(row, place), board)
-    sent[...] = board
-
-    kept = [low * mask[:, :128], high * mask[:, 128:]]
-    back = [dot3(right, split(part)) for part in kept]
+    return board
+
+
+def project_kernel(grads, th, tl, out):
     for q in range(4):
-        piece = back[q // 2][:, (q % 2) * 64:(q % 2) * 64 + 64]
+        part = grads[:, q * 256:(q + 1) * 256]
+        out[:, q * 64:(q + 1) * 64] = (dot(part, th[...]) + dot(part, tl[...])) * SCALE
+
+
+def nt(x, y):
+    return lax.dot_general(x, y, (((1,), (1,)), ((), ())), preferred_element_type=F32)
+
+
+def inputs_kernel(inputs, lh, ll, high, low):
+    left = jnp.concatenate([lh[...], ll[...]], axis=0)
+    for z in range(4):
+        for x in range(4):
+            for c in range(2):
+                at = ((z * 4 + x) * 2 + c) * 128
+                both = nt(left, inputs[at:at + 128, :])
+                part = split(both[:64] + both[64:])
+                to = (x * 4 + z) * 128
+                high[c, :, to:to + 128] = part[0]
+                low[c, :, to:to + 128] = part[1]
+
+
+def moment_kernel(momentum, lh, ll, th, tl, out):
+    left, right = (lh[...], ll[...]), (th[...], tl[...])
+    half = dot3(left, split(0.999 * momentum[...]))
+    for q in range(4):
+        out[:, q * 64:(q + 1) * 64] = dot3(split(half[:, q * 256:(q + 1) * 256]), right)
+
+
+def contract(high, low, side, source):
+    xh, xl = split(source)
+    both = dot(jnp.concatenate([high[side], low[side]], axis=0), xh)
+    return (both[:64] + (both[64:] + dot(high[side], xl))) * (1.0 / SCALE)
+
+
+def near_kernel(core, high, low, own, kept, out):
+    out[...] = kept[...] + contract(high, low, core[0], own[...])
+
+
+def far_kernel(core, high, low, other, near, col_index, row_pick, slot_row, slot_lane, coef, sent):
+    total = near[...] + contract(high, low, 1 - core[0], other[...])
+    coef[...] = total
+    board = select(total[:, :128], total[:, 128:], col_index, row_pick, slot_row, slot_lane)
+    for r in range(16):
+        sent[r * 32:(r + 1) * 32, :] = board
+
+
+def turn_kernel(inputs, out):
+    for t in range(8):
+        out[:, t * 512:(t + 1) * 512] = inputs[t * 512:(t + 1) * 512, :].T
+
+
+def final_kernel(turned, grads, base, out):
+    step = pl.program_id(0)
+
+    @pl.when(step == 0)
+    def _():
+        out[...] = base[...]
+
+    out[...] += dot(turned[...], grads[...])
+
+
+def base_kernel(momentum, coef, mask, lh, ll, th, tl, out):
+    left, right = (lh[...], ll[...]), (th[...], tl[...])
+    back = dot3(right, split(coef[...] * mask[...]))
+    for q in range(4):
         cols = slice(q * 256, (q + 1) * 256)
-        new[:, cols] = whole[:, cols] - dot3(split(piece), left)
+        out[:, cols] = 0.999 * momentum[:, cols] - dot3(split(back[:, q * 64:(q + 1) * 64]), left)
 
 
 def decode_kernel(received, index, kh, kl, out, first, second):
@@ -111,16 +169,21 @@
     return [pl.BlockSpec(memory_space=pltpu.VMEM)] * n
 
 
-def encode(fresh, tables):
-    lh, ll = split_np(block_basis())
+def call(kernel, shapes, *args, scalars=0):
+    scalar = [pl.BlockSpec(memory_space=pltpu.SMEM)] * scalars
+    many = isinstance(shapes, tuple)
     return pl.pallas_call(
-        encode_kernel,
-        out_shape=(jax.ShapeDtypeStruct((ROWS, WIDTH), F32), jax.ShapeDtypeStruct((32, 128), F32)),
-        in_specs=vmem(10),
-        out_specs=tuple(vmem(2)),
+        kernel,
+        out_shape=shapes,
+        in_specs=scalar + vmem(len(args) - scalars),
+        out_specs=tuple(vmem(len(shapes))) if many else vmem(1)[0],
         compiler_params=pltpu.CompilerParams(vmem_limit_bytes=40 << 20),
-        name="encode",
-    )(fresh, lh, ll, lh.T.copy(), ll.T.copy(), *tables)
+        name=kernel.__name__,
+    )(*args)
+
+
+def sds(shape, dtype=F32):
+    return jax.ShapeDtypeStruct(shape, dtype)
 
 
 def decode(received, index):
@@ -167,28 +230,72 @@
     return jnp.transpose(index, (1, 0, 2, 3)).reshape(64, BAND * BAND)
 
 
+def shard(z, x, c):
+    return (z * 4 + x) * 2 + c
+
+
+ALONG_X = [[shard(z, x, c) for x in range(4)] for z in range(4) for c in range(2)]
+ALONG_Z = [[shard(z, x, c) for z in range(4)] for x in range(4) for c in range(2)]
+OTHER_CORE = [(i, i ^ 1) for i in range(32)]
+
+
+def gather(block, groups):
+    copies = jnp.broadcast_to(block[None], (4,) + block.shape).reshape((4 * block.shape[0],) + block.shape[1:])
+    return lax.all_to_all(copies, "shard", 0, 0, tiled=True, axis_index_groups=groups)
+
+
 def body(activations, key_grads, momentum, freq_rows, freq_cols, dispatch):
     position = lax.axis_index("shard")
-    grad = lax.dot_general(
-        activations,
-        lax.all_gather(key_grads, "shard", axis=0, tiled=True),
-        (((0,), (0,)), ((), ())),
-        preferred_element_type=F32,
-    )
-    fresh = 0.999 * momentum + grad
+    lh, ll = split_np(block_basis())
+    th, tl = lh.T.copy(), ll.T.copy()
+    all_grads = lax.all_gather(key_grads, "shard", axis=0, tiled=True)
+
+    band = call(project_kernel, sds((128, 256)), key_grads, th, tl).astype(jnp.float16)
+    along_z = gather(band, ALONG_Z)
+
     my_rows = lax.dynamic_slice_in_dim(freq_rows, position * 4, 4, 0)
     my_cols = lax.dynamic_slice_in_dim(freq_cols, position * 4, 4, 0)
     slots = lax.dynamic_slice_in_dim(dispatch, position, 1, 0).reshape(64)
-    new_momentum, board = encode(fresh, sender_tables(my_rows, my_cols, slots))
-
-    own = lax.dynamic_slice_in_dim(dispatch, position * 2, 2, 1)
-    span_ids = (jnp.arange(32, dtype=jnp.int32)[:, None] * 64 + own).reshape(-1)
+    tables = sender_tables(my_rows, my_cols, slots)
+    kept = call(moment_kernel, sds((64, 256)), momentum, lh, ll, th, tl)
+    along_z, kept, (mask, *picks) = lax.optimization_barrier((along_z, kept, tables))
+    own = gather(along_z, ALONG_X)
+
+    high, low = call(inputs_kernel, (sds((2, 64, 2048), BF16),) * 2, activations, lh, ll)
+    own_slots = lax.dynamic_slice_in_dim(dispatch, position * 2, 2, 1)
+    span_ids = (jnp.arange(32, dtype=jnp.int32)[:, None] * 64 + own_slots).reshape(-1)
     own_rows = freq_rows.reshape(-1, K)[span_ids].reshape(32, 2, K)
     own_cols = freq_cols.reshape(-1, K)[span_ids].reshape(32, 2, K)
     index = owner_table(own_rows, own_cols)
-    board = jnp.broadcast_to(board[None], (16, 32, 128)).reshape(512, 128)
+    own, high, low, index = lax.optimization_barrier((own, high, low, index))
+
+    other = lax.ppermute(own, "shard", OTHER_CORE)
+    core = (position % 2).astype(jnp.int32).reshape(1)
+    near = call(near_kernel, sds((64, 256)), core, high, low, own.astype(F32), kept, scalars=1)
+    coef, board = call(
+        far_kernel, (sds((64, 256)), sds((512, 128))),
+        core, high, low, other.astype(F32), near, *picks, scalars=1,
+    )
     received = lax.all_to_all(board, ("rep", "shard"), 0, 0, tiled=True)
+    base = call(base_kernel, sds((ROWS, WIDTH)), momentum, coef, mask, lh, ll, th, tl)
+    turned = call(turn_kernel, sds((ROWS, 4096), BF16), activations)
+    received, base, turned = lax.optimization_barrier((received, base, turned))
     update = decode(received, index)
+
+    new_momentum = pl.pallas_call(
+        final_kernel,
+        grid=(8,),
+        out_shape=sds((ROWS, WIDTH)),
+        in_specs=[
+            pl.BlockSpec((ROWS, 512), lambda t: (0, t)),
+            pl.BlockSpec((512, WIDTH), lambda t: (t, 0)),
+            pl.BlockSpec((ROWS, WIDTH), lambda t: (0, 0)),
+        ],
+        out_specs=pl.BlockSpec((ROWS, WIDTH), lambda t: (0, 0)),
+        compiler_params=pltpu.CompilerParams(vmem_limit_bytes=40 << 20),
+        cost_estimate=pl.CostEstimate(flops=2 * 4096 * ROWS * WIDTH, bytes_accessed=14 << 20, transcendentals=0),
+        name="final",
+    )(turned, all_grads, base)
     return (new_momentum, update)
 
 

time: 141 us -> 136 us (0.965); the launches traced: 141 us -> 135 us
  waiting for transfers between devices: 85.2 us -> 31.3 us
  local copies, waits for them, and re-layouts: 15.4 us -> 36.7 us
  starting transfers between devices: 14.8 us -> 34.5 us
  Pallas kernels: 4.5 us -> 11.6 us
  matrix products: 5.73 us -> 0 us
  other arithmetic: 1.01 us -> 6.03 us
    all_gather x1, waiting for transfers between devices: 68.2 us -> 0.01 us  [body(): all_grads = lax.all_gather(key_grads, 'shard', axis=0, tiled=True)]
    all_to_all x0 -> x2, waiting for transfers between devices: none -> 21.2 us  [gather(): lax.all_to_all(copies, 'shard', 0, 0, tiled=True, axis_index_groups=groups)]
    unnamed x21 -> x53, local copies, waits for them, and re-layouts: 7.89 us -> 21.1 us
    all_to_all x0 -> x2, starting transfers between devices: none -> 12.1 us  [gather(): lax.all_to_all(copies, 'shard', 0, 0, tiled=True, axis_index_groups=groups)]
    all_to_all x1, waiting for transfers between devices: 16.3 us -> 8.92 us  [body(): received = lax.all_to_all(board, ('rep', 'shard'), 0, 0, tiled=True)]
    pallas_call x1 -> x8, Pallas kernels: 2.42 us -> 9.48 us  [the longest x1 4.82 us: body(): pl.pallas_call(final_kernel, grid=(8,), out_shape=sds((ROWS, WIDTH)), in_...]
    ppermute x0 -> x1, starting transfers between devices: none -> 5.96 us  [body(): other = lax.ppermute(own, 'shard', OTHER_CORE)]
    dot_general x1 -> x0, matrix products: 5.73 us -> none  [body(): lax.dot_general(activations, lax.all_gather(key_grads, 'shard', axis=0, t...]
  transfers between devices with their start and end apart: 2 -> 5, of which waited for: 2 -> 3; matrix products, arithmetic and copies ran while one was open for 9% -> 19% of each run, Pallas kernels for 0% -> 5%
where the time goes in v2:
time: 136 us; the launch traced here: 135 us
  local copies, waits for them, and re-layouts  36.7 us (27%)
  starting transfers between devices  34.5 us (25%)
  waiting for transfers between devices  31.3 us (23%)
  between operations  14.4 us (11%)
  Pallas kernels  11.6 us (9%)
  other arithmetic  6.03 us (4%)
    all_to_all x2, waiting for transfers between devices, gather(): lax.all_to_all(copies, 'shard', 0, 0, tiled=True, axis_index_groups=groups)  21.2 us
    unnamed x53, local copies, waits for them, and re-layouts  21.1 us
    all_to_all x1, starting transfers between devices, body(): received = lax.all_to_all(board, ('rep', 'shard'), 0, 0, tiled=True)  16.5 us
    all_to_all x2, starting transfers between devices, gather(): lax.all_to_all(copies, 'shard', 0, 0, tiled=True, axis_index_groups=groups)  12.1 us
    all_to_all x1, waiting for transfers between devices, body(): received = lax.all_to_all(board, ('rep', 'shard'), 0, 0, tiled=True)  8.92 us
    ppermute x1, starting transfers between devices, body(): other = lax.ppermute(own, 'shard', OTHER_CORE)  5.96 us
    pallas_call x1, Pallas kernels, body(): pl.pallas_call(final_kernel, grid=(8,), out_shape=sds((ROWS, WIDTH)), in_...  4.82 us
    pallas_call x7, Pallas kernels, call(): pl.pallas_call(kernel, out_shape=shapes, in_specs=scalar + vmem(len(args)...  4.66 us
  transfers between devices with their start and end apart: 5, of which 3 were waited for; matrix products, arithmetic and copies ran while one was open for 19% of the time, Pallas kernels for 5%

profile of v2, /device:TPU:1, one launch (start us, length us, event | category | flops | bytes accessed | tf_op | source)
XLA Modules:
  0.0 134.6 jit_solution(6106235564721175323)
XLA Ops:
  11.6 7.8 %all-to-all-start = ((f16[4,128,256]{2,1,0:T(8,128)(2,1)}), f16[4,128,256]{2,1,0:T(8,128)(2,1)}, u32[]{:S(2)}, u32[]{:S(2)}) async-start(f16[4,128,256]{2,1,0:T(8,128)(2,1)} %broadcast_in_dim.27), calls=%async_computation | async-start | bytes 524288 | tf_op jit(solution)/shard_map/all_to_all | solution.py:244
  20.8 1.4 %copy.75 = s32[128,16,8]{2,1,0:T(8,128)} copy(s32[128,16,8]{0,2,1:T(8,128)S(1)} %copy-done.23) | data formatting | bytes 131072 | tf_op args[4]
  22.2 2.4 %copy.72 = s32[128,16,8]{2,1,0:T(8,128)} copy(s32[128,16,8]{0,2,1:T(8,128)} %param.15) | data formatting | bytes 131072 | tf_op args[3]
  26.2 1.9 %reshape.233.mask = f32[64,256]{1,0:T(8,128)} reshape(f32[4,16,16,16]{3,2,1,0:T(8,128)} %and_convert_fusion) | data formatting | bytes 131072 | tf_op jit(solution)/shard_map/convert_element_type | solution.py:207
  29.3 1.1 reshape.227.row_pick
  32.3 1.8 %gather_fusion.1 = s32[64,8]{1,0:T(8,128)S(1)} fusion(s32[2048,8]{1,0:T(8,128)} %bitcast.31, s32[1024]{0:T(1024)S(1)} %pad_clamp_fusion), kind=kCustom, calls=%fused_computation.1 | custom fusion | bytes 4352 | tf_op jit(solution)/shard_map/gather | solution.py:268
  34.3 1.8 %gather_fusion = s32[64,8]{1,0:T(8,128)S(1)} fusion(s32[2048,8]{1,0:T(8,128)} %bitcast.30, s32[1024]{0:T(1024)S(1)} %pad_clamp_fusion), kind=kCustom, calls=%fused_computation | custom fusion | bytes 4352 | tf_op jit(solution)/shard_map/gather | solution.py:267
  36.9 2.0 %broadcast_in_dim.31 = f16[4,512,256]{2,1,0:T(8,128)(2,1)} broadcast(f16[512,256]{1,0:T(8,128)(2,1)} %bitcast.1), dimensions={1,2} | broadcast | bytes 1310720 | tf_op jit(solution)/shard_map/broadcast_in_dim | solution.py:243
  38.9 4.3 %all-to-all-start.1 = ((f16[4,512,256]{2,1,0:T(8,128)(2,1)}), f16[4,512,256]{2,1,0:T(8,128)(2,1)}, u32[]{:S(2)}, u32[]{:S(2)}) async-start(f16[4,512,256]{2,1,0:T(8,128)(2,1)} %broadcast_in_dim.31), calls=%async_computation.1 | async-start | bytes 2097152 | tf_op jit(solution)/shard_map/all_to_all | solution.py:244
  43.3 1.6 %and_select_fusion = s32[2,32,16,16]{1,0,3,2:T(2,128)} fusion(pred[2,32,16]{1,0,2:T(4,128)(4,1)S(1)} %copy.77, pred[2,32,16]{1,0,2:T(4,128)(4,1)} %copy.74, s32[2,32,16]{1,0,2:T(2,128)S(1)} %copy.79, s32[2,32,16]{1,0,2:T(2,128)S(1)} %copy.78), kind=kLoop, calls=%fused_computation.2 | loop fusion | flops 49152 | bytes 75776 | tf_op jit(solution)/shard_map/jit(_where)/select_n | solution.py:229
  44.9 1.8 %select_n.86 = s32[64,256]{0,1:T(8,128)} reshape(s32[2,32,16,16]{1,0,3,2:T(2,128)} %and_select_fusion) | data formatting | bytes 131072 | tf_op jit(solution)/shard_map/jit(_where)/select_n | solution.py:229
  46.6 21.1 %all-to-all-done.1 = f16[4,512,256]{2,1,0:T(8,128)(2,1)} async-done(((f16[4,512,256]{2,1,0:T(8,128)(2,1)}), f16[4,512,256]{2,1,0:T(8,128)(2,1)}, u32[]{:S(2)}, u32[]{:S(2)}) %all-to-all-start.1) | async-done | bytes 1048608 | tf_op jit(solution)/shard_map/all_to_all | solution.py:244
  67.8 6.0 %collective-permute-start = (f16[2048,256]{1,0:T(8,128)(2,1)}, f16[2048,256]{1,0:T(8,128)(2,1)}, u32[]{:S(2)}, u32[]{:S(2)}) collective-permute-start(f16[2048,256]{1,0:T(8,128)(2,1)} %bitcast.6), channel_id=1, source_target_pairs={{0,1},{1,0},{2,3},{3,2},{4,5},{5,4},{6,7},{7,6},{8,9},{9,8},{10,11... | collective-permute-start | bytes 3145736 | tf_op jit(solution)/shard_map/ppermute | solution.py:272
  73.9 1.4 %convert_element_type.19.own = f32[2048,256]{1,0:T(8,128)S(1)} convert(f16[2048,256]{1,0:T(8,128)(2,1)} %bitcast.6) | non-fusion elementwise | flops 524288 | bytes 3145728 | tf_op jit(solution)/shard_map/convert_element_type | solution.py:274
  76.4 1.4 %convert_element_type.18.other = f32[2048,256]{1,0:T(8,128)S(1)} convert(f16[2048,256]{1,0:T(8,128)(2,1)} %collective-permute-done) | non-fusion elementwise | flops 524288 | bytes 3145728 | tf_op jit(solution)/shard_map/convert_element_type | solution.py:277
  80.1 16.5 %all-to-all-start.2 = ((f32[512,1,128]{2,1,0:T(1,128)}), f32[512,1,128]{2,1,0:T(1,128)S(1)}, u32[]{:S(2)}, u32[]{:S(2)}) async-start(f32[512,1,128]{2,1,0:T(1,128)} %bitcast.29), calls=%async_computation.2 | async-start | bytes 524288 | tf_op jit(solution)/shard_map/all_to_all | solution.py:279
  97.2 1.4 %copy-done.2 = bf16[256,4096]{1,0:T(8,128)(2,1)} copy-done((bf16[256,4096]{1,0:T(8,128)(2,1)}, bf16[256,4096]{1,0:T(8,128)(2,1)S(1)}, u32[]{:S(2)}) %copy-start.2) | copy-done | bytes 2097176
  99.3 1.2 copy-done.5
  104.5 8.9 %all-to-all-done.2 = f32[512,1,128]{2,1,0:T(1,128)S(1)} async-done(((f32[512,1,128]{2,1,0:T(1,128)}), f32[512,1,128]{2,1,0:T(1,128)S(1)}, u32[]{:S(2)}, u32[]{:S(2)}) %all-to-all-start.2) | async-done | bytes 262176 | tf_op jit(solution)/shard_map/all_to_all | solution.py:279
  113.4 1.6 %copy-done.6 = bf16[256,4096]{1,0:T(8,128)(2,1)S(1)} copy-done((bf16[256,4096]{1,0:T(8,128)(2,1)S(1)}, bf16[256,4096]{1,0:T(8,128)(2,1)}, u32[]{:S(2)}) %copy-start.6) | copy-done | bytes 2097176
  115.0 1.6 %copy-done.7 = bf16[256,4096]{1,0:T(8,128)(2,1)S(1)} copy-done((bf16[256,4096]{1,0:T(8,128)(2,1)S(1)}, bf16[256,4096]{1,0:T(8,128)(2,1)}, u32[]{:S(2)}) %copy-start.7) | copy-done | bytes 2097176
  117.4 2.1 %decode.1 = bf16[64,4096]{1,0:T(8,128)(2,1)} custom-call(f32[512,128]{1,0:T(8,128)S(1)} %bitcast.28, s32[64,256]{1,0:T(8,128)S(1)} %copy-done.17, bf16[256,4096]{1,0:T(8,128)(2,1)S(1)} %copy-done.6, bf16[256,4096]{1,0:T(8,128)(2,1)S(1)} %copy-done.7), custom_call_target="tpu_custom_call" | custom-call | tf_op jit(solution)/shard_map/decode/pallas_call | solution.py:191
  119.5 3.4 %copy-done = bf16[4096,1024]{1,0:T(8,128)(2,1)S(1)} copy-done((bf16[4096,1024]{1,0:T(8,128)(2,1)S(1)}, bf16[4096,1024]{1,0:T(8,128)(2,1)}, u32[]{:S(2)}) %copy-start) | copy-done | bytes 8388632
  122.9 4.8 %final.1 = f32[256,1024]{1,0:T(8,128)} custom-call(bf16[256,4096]{1,0:T(8,128)(2,1)S(1)} %copy-done.3, bf16[4096,1024]{1,0:T(8,128)(2,1)S(1)} %copy-done, f32[256,1024]{1,0:T(8,128)S(1)} %base_kernel.1.base), custom_call_target="tpu_custom_call" | custom-call | flops 2147483648 | bytes 14680064 | tf_op jit(solution)/shard_map/final/pallas_call | solution.py:285
  (100 shorter events, 20.9 us)
Async XLA Ops:
  7.2 13.6 %copy-start.23 = (s32[128,16,8]{0,2,1:T(8,128)S(1)}, s32[128,16,8]{0,2,1:T(8,128)}, u32[]{:S(2)}) copy-start(s32[128,16,8]{0,2,1:T(8,128)} %param.16) | copy-start | bytes 196612
  7.2 112.4 %all-gather.2.cloned.1.call-start = ((), (), s32[]{:S(2)}) async-start(), calls=%async_computation.3 | async-start | bytes 8650752 | tf_op jit(solution)/shard_map/all_gather | solution.py:251
  7.9 1.0 copy-start.8
  8.9 0.8 copy-start.9
  9.7 0.8 copy-start.11
  11.6 25.2 %all-to-all-start = ((f16[4,128,256]{2,1,0:T(8,128)(2,1)}), f16[4,128,256]{2,1,0:T(8,128)(2,1)}, u32[]{:S(2)}, u32[]{:S(2)}) async-start(f16[4,128,256]{2,1,0:T(8,128)(2,1)} %broadcast_in_dim.27), calls=%async_computation | async-start | bytes 524288 | tf_op jit(solution)/shard_map/all_to_all | solution.py:244
  20.7 9.6 %copy-start.24 = (s32[32,64]{1,0:T(8,128)S(1)}, s32[32,64]{1,0:T(8,128)}, u32[]{:S(2)}) copy-start(s32[32,64]{1,0:T(8,128)} %param.17) | copy-start | bytes 24580
  20.7 9.8 %copy-start.4 = (f32[256,1024]{1,0:T(8,128)S(1)}, f32[256,1024]{1,0:T(8,128)}, u32[]{:S(2)}) copy-start(f32[256,1024]{1,0:T(8,128)} %momentum.3) | copy-start | bytes 3145732
  20.7 9.8 %copy-start.10 = (bf16[256,64]{1,0:T(8,128)(2,1)S(1)}, bf16[256,64]{1,0:T(8,128)(2,1)}, u32[]{:S(2)}) copy-start(bf16[256,64]{1,0:T(8,128)(2,1)} %constant.89.clone.th) | copy-start | bytes 98308
  20.8 9.8 %copy-start.12 = (bf16[256,64]{1,0:T(8,128)(2,1)S(1)}, bf16[256,64]{1,0:T(8,128)(2,1)}, u32[]{:S(2)}) copy-start(bf16[256,64]{1,0:T(8,128)(2,1)} %constant.90.clone.tl) | copy-start | bytes 98308
  20.8 9.8 %copy-start.13 = (bf16[64,256]{1,0:T(8,128)(2,1)S(1)}, bf16[64,256]{1,0:T(8,128)(2,1)}, u32[]{:S(2)}) copy-start(bf16[64,256]{1,0:T(8,128)(2,1)} %constant.91.clone.lh) | copy-start | bytes 98308
  20.8 9.8 %copy-start.15 = (bf16[64,256]{1,0:T(8,128)(2,1)S(1)}, bf16[64,256]{1,0:T(8,128)(2,1)}, u32[]{:S(2)}) copy-start(bf16[64,256]{1,0:T(8,128)(2,1)} %constant.92.clone.ll) | copy-start | bytes 98308
  22.2 9.2 %copy-start.1 = (bf16[4096,256]{1,0:T(8,128)(2,1)S(1)}, bf16[4096,256]{1,0:T(8,128)(2,1)}, u32[]{:S(2)}) copy-start(bf16[4096,256]{1,0:T(8,128)(2,1)} %inputs.3) | copy-start | bytes 6291460
  38.9 28.9 %all-to-all-start.1 = ((f16[4,512,256]{2,1,0:T(8,128)(2,1)}), f16[4,512,256]{2,1,0:T(8,128)(2,1)}, u32[]{:S(2)}, u32[]{:S(2)}) async-start(f16[4,512,256]{2,1,0:T(8,128)(2,1)} %broadcast_in_dim.31), calls=%async_computation.1 | async-start | bytes 2097152 | tf_op jit(solution)/shard_map/all_to_all | solution.py:244
  67.8 8.6 %collective-permute-start = (f16[2048,256]{1,0:T(8,128)(2,1)}, f16[2048,256]{1,0:T(8,128)(2,1)}, u32[]{:S(2)}, u32[]{:S(2)}) collective-permute-start(f16[2048,256]{1,0:T(8,128)(2,1)} %bitcast.6), channel_id=1, source_target_pairs={{0,1},{1,0},{2,3},{3,2},{4,5},{5,4},{6,7},{7,6},{8,9},{9,8},{10,11... | collective-permute-start | bytes 3145736 | tf_op jit(solution)/shard_map/ppermute | solution.py:272
  80.1 33.3 %all-to-all-start.2 = ((f32[512,1,128]{2,1,0:T(1,128)}), f32[512,1,128]{2,1,0:T(1,128)S(1)}, u32[]{:S(2)}, u32[]{:S(2)}) async-start(f32[512,1,128]{2,1,0:T(1,128)} %bitcast.29), calls=%async_computation.2 | async-start | bytes 524288 | tf_op jit(solution)/shard_map/all_to_all | solution.py:279
  96.6 2.0 %copy-start.22 = (s32[64,256]{0,1:T(8,128)S(1)}, s32[64,256]{0,1:T(8,128)}, u32[]{:S(2)}) copy-start(s32[64,256]{0,1:T(8,128)} %select_n.86) | copy-start | bytes 196612
  97.2 1.4 %copy-start.2 = (bf16[256,4096]{1,0:T(8,128)(2,1)}, bf16[256,4096]{1,0:T(8,128)(2,1)S(1)}, u32[]{:S(2)}) copy-start(bf16[256,4096]{1,0:T(8,128)(2,1)S(1)} %turn_kernel.1.turned) | copy-start | bytes 6291460
  99.3 1.2 copy-start.5
  113.4 1.6 %copy-start.6 = (bf16[256,4096]{1,0:T(8,128)(2,1)S(1)}, bf16[256,4096]{1,0:T(8,128)(2,1)}, u32[]{:S(2)}) copy-start(bf16[256,4096]{1,0:T(8,128)(2,1)} %constant.93.clone.kh) | copy-start | bytes 6291460
  115.0 1.6 %copy-start.7 = (bf16[256,4096]{1,0:T(8,128)(2,1)S(1)}, bf16[256,4096]{1,0:T(8,128)(2,1)}, u32[]{:S(2)}) copy-start(bf16[256,4096]{1,0:T(8,128)(2,1)} %constant.94.clone.kl) | copy-start | bytes 6291460
  116.6 0.8 copy-start.17
  117.4 2.1 %copy-start.3 = (bf16[256,4096]{1,0:T(8,128)(2,1)S(1)}, bf16[256,4096]{1,0:T(8,128)(2,1)}, u32[]{:S(2)}) copy-start(bf16[256,4096]{1,0:T(8,128)(2,1)} %copy-done.2) | copy-start | bytes 6291460
  119.5 3.4 %copy-start = (bf16[4096,1024]{1,0:T(8,128)(2,1)S(1)}, bf16[4096,1024]{1,0:T(8,128)(2,1)}, u32[]{:S(2)}) copy-start(bf16[4096,1024]{1,0:T(8,128)(2,1)} %all-gather.2.cloned.1.call-done.grads) | copy-start | bytes 25165828
  (6 other events, 4.5 us)
Sparse Core Ops, SparseCore 0:
  10.2 88.9 all-gather.1

commit v3 on v1

v3 whole, which is shorter than its diff:
```python
import jax
import jax.numpy as jnp
import numpy as np
from jax import lax
from jax.experimental import pallas as pl
from jax.experimental.pallas import tpu as pltpu
from jax.sharding import PartitionSpec as P

CH = 64
K = 8
BAND = 16
ROWS = 256
WIDTH = 1024
TOKENS = 4096
LEVELS = 32000.0
SENT = 144
F32 = jnp.float32
BF16 = jnp.bfloat16
I32 = jnp.int32


def band_table():
    frequency = np.arange(BAND)[:, None]
    sample = np.arange(CH)[None, :]
    scales = np.where(frequency == 0, np.sqrt(1.0 / CH), np.sqrt(2.0 / CH))
    return scales * np.cos(np.pi * (2.0 * sample + 1.0) * frequency / (2.0 * CH))


def split_np(x):
    hi = x.astype(np.float32).astype(jnp.bfloat16)
    lo = (x - hi.astype(np.float64)).astype(np.float32).astype(jnp.bfloat16)
    return hi, lo


def block_basis():
    return np.kron(np.eye(4), band_table())


def pair_basis():
    return np.kron(band_table(), band_table())


def split(x):
    hi = x.astype(BF16)
    return hi, (x - hi.astype(F32)).astype(BF16)


def dot(x, y):
    return lax.dot_general(x, y, (((1,), (0,)), ((), ())), preferred_element_type=F32)


def nt(x, y):
    return lax.dot_general(x, y, (((1,), (1,)), ((), ())), preferred_element_type=F32)


def dot3(x, y):
    (xh, xl), (yh, yl) = x, y
    return dot(xh, yh) + (dot(xh, yl) + dot(xl, yh))


def lanes(x, index):
    return jnp.take_along_axis(x, index, axis=1)


def iota(shape, axis):
    return lax.broadcasted_iota(I32, shape, axis)


def power(exponent):
    return jnp.exp2(exponent).astype(BF16).astype(F32)


def project_kernel(grads, th, tl, out):
    parts = []
    for q in range(4):
        part = grads[:, q * 256:(q + 1) * 256]
        parts.append(dot(part, th[...]) + dot(part, tl[...]))
    band = jnp.concatenate(parts, axis=1)
    top = jnp.maximum(jnp.max(jnp.abs(band), axis=1, keepdims=True), 1e-35)
    exponent = jnp.broadcast_to(jnp.ceil(jnp.log2(top)), (128, 128))
    code = jnp.floor(band * (power(-exponent[:, :1]) * LEVELS) + 0.5)
    scales = jnp.concatenate([exponent.T[:16]] * 2, axis=1)
    sent = jnp.concatenate([code, scales], axis=0).astype(I32).astype(jnp.int16)
    for k in range(4):
        out[k * SENT:(k + 1) * SENT, :] = sent


def tables_kernel(place, freq_rows, freq_cols, dispatch, mask, col_index, row_pick, slot_row, slot_lane, index):
    s = place[0]
    rows = freq_rows[...].reshape(128, 128).astype(F32).astype(BF16)
    cols = freq_cols[...].reshape(128, 128).astype(F32).astype(BF16)
    sub, lane = iota((8, 128), 0), iota((8, 128), 1)
    pick = jnp.where((lane == s * 4 + sub) & (sub < 4), 1.0, 0.0).astype(BF16)
    my_rows = nt(pick, rows).astype(I32)
    my_cols = nt(pick, cols).astype(I32)
    col_index[...] = my_cols + ((lane >> 3) & 7) * BAND
    for i in range(K):
        value = lanes(my_rows, (lane & 120) + i)
        for a in range(4):
            row_pick[a * K + i:a * K + i + 1, :] = value[a:a + 1]
    f1 = iota((BAND, 128), 0)
    for h in range(2):
        source = h * 64 + (lane >> 4) * K
        hit = jnp.zeros((8, 128), I32)
        for j in range(K):
            hit += jnp.where(lanes(my_cols, source + j) == (lane & 15), 1, 0)
        values = [lanes(my_rows, source + i) for i in range(K)]
        for a in range(4):
            found = jnp.zeros((BAND, 128), I32)
            for value in values:
                found += jnp.where(jnp.broadcast_to(value[a:a + 1], (BAND, 128)) == f1, 1, 0)
            both = found * jnp.broadcast_to(hit[a:a + 1], (BAND, 128))
            mask[a * BAND:(a + 1) * BAND, h * 128:(h + 1) * 128] = both.astype(F32)

    def doubled(x):
        return jnp.concatenate([x, x], axis=1)

    sub, lane = iota((32, 128), 0), iota((32, 128), 1)
    mine = jnp.broadcast_to(doubled(dispatch[pl.ds(s, 1), :]), (32, 128))
    slot = lanes(mine, sub * 2 + (lane >> 6))
    slot_row[...] = (slot >> 4) * K + ((lane >> 3) & 7)
    slot_lane[...] = (slot & 15) * K + (lane & 7)

    whole = doubled(dispatch[...])
    owned = [lanes(whole, jnp.zeros((32, 128), I32) + (s * 2 + k)) for k in range(2)]
    owned = jnp.concatenate(owned, axis=0)
    sub, lane = iota((64, 128), 0), iota((64, 128), 1)
    pick = jnp.where(lane == (sub & 31) * 4 + (owned >> 4), 1.0, 0.0).astype(BF16)
    own_rows = nt(pick, rows).astype(I32)
    own_cols = nt(pick, cols).astype(I32)
    first = (owned & 15) * K
    row_values = [lanes(own_rows, first + i) for i in range(K)]
    col_values = [lanes(own_cols, first + i) for i in range(K)]

    def at(values, frequency):
        seen, where = jnp.zeros((64, 128), I32), jnp.zeros((64, 128), I32)
        for i, value in enumerate(values):
            same = value == frequency
            seen += jnp.where(same, 1, 0)
            where += jnp.where(same, i, 0)
        return seen, where

    col_seen, col_at = at(col_values, lane & 15)
    start = (sub >> 5) * 64
    for h in range(2):
        row_seen, row_at = at(row_values, h * 8 + (lane >> 4))
        found = start + row_at * K + col_at
        index[:, h * 128:(h + 1) * 128] = jnp.where(row_seen * col_seen > 0, found, -1)


def prepare_kernel(inputs, momentum, lh, ll, th, tl, high, low, kept, turned):
    both_basis = jnp.concatenate([lh[...], ll[...]], axis=0)
    for z in range(4):
        for x in range(4):
            for c in range(2):
                at = ((z * 4 + x) * 2 + c) * 128
                block = inputs[at:at + 128, :]
                both = nt(both_basis, block)
                part = split(both[:64] + both[64:])
                to = (x * 4 + z) * 128
                high[c, :, to:to + 128] = part[0]
                low[c, :, to:to + 128] = part[1]
                turned[:, at:at + 128] = block.T
    left, right = (lh[...], ll[...]), (th[...], tl[...])
    half = dot3(left, split(0.999 * momentum[...]))
    for q in range(4):
        kept[:, q * 64:(q + 1) * 64] = dot3(split(half[:, q * 256:(q + 1) * 256]), right)


def contract(high, low, side, source):
    total = jnp.zeros((64, 256), F32)
    for k in range(16):
        at, to = k * SENT, k * 128
        xh, xl = split(source[at:at + 128, :].astype(I32).astype(F32))
        scale = power(source[at + 128:at + 144, :].astype(I32).astype(F32)[:1, :128]).astype(BF16)
        left = jnp.concatenate([high[side, :, to:to + 128], low[side, :, to:to + 128]], axis=0)
        left = left * jnp.broadcast_to(scale, (128, 128))
        both = dot(left, xh)
        total += both[:64] + (both[64:] + dot(left[:64], xl))
    return total * (1.0 / LEVELS)


def near_kernel(place, high, low, own, kept, out):
    out[...] = kept[...] + contract(high, low, place[0] & 1, own)


def select(low, high, col_index, row_pick, slot_row, slot_lane):
    lane = iota((BAND, 128), 1)
    picked = []
    for a in range(4):
        rows = slice(a * BAND, (a + 1) * BAND)
        index = jnp.broadcast_to(col_index[a:a + 1, :], (BAND, 128))
        cols = jnp.where(lane < 64, lanes(low[rows], index), lanes(high[rows], index))
        want = row_pick[a * K:(a + 1) * K, :]
        total = jnp.zeros((K, 128), F32)
        for f in range(BAND):
            total = jnp.where(want == f, jnp.broadcast_to(cols[f:f + 1], (K, 128)), total)
        picked.append(total)
    code, place = slot_row[...], slot_lane[...]
    board = jnp.zeros((32, 128), F32)
    for a in range(4):
        for i in range(K):
            row = jnp.broadcast_to(picked[a][i:i + 1], (32, 128))
            board = jnp.where(code == a * K + i, lanes(row, place), board)
    return board


def far_kernel(place, high, low, other, near, col_index, row_pick, slot_row, slot_lane, coef, sent):
    total = near[...] + contract(high, low, 1 - (place[0] & 1), other)
    coef[...] = total
    board = select(total[:, :128], total[:, 128:], col_index, row_pick, slot_row, slot_lane)
    for r in range(16):
        sent[r * 32:(r + 1) * 32, :] = board


def final_kernel(turned, grads, momentum, coef, mask, lh, ll, th, tl, out, done):
    @pl.when(pl.program_id(0) == 0)
    def _():
        left, right = (lh[...], ll[...]), (th[...], tl[...])
        back = dot3(right, split(coef[...] * mask[...]))
        for q in range(4):
            cols = slice(q * 256, (q + 1) * 256)
            out[:, cols] = 0.999 * momentum[:, cols] - dot3(split(back[:, q * 64:(q + 1) * 64]), left)
        done[...] = jnp.zeros((8, 128), F32)

    out[...] += dot(turned[...], grads[...])


def decode_kernel(received, index, kh, kl, done, out, first, second):
    @pl.when(pl.program_id(0) == 0)
    def _():
        total = received[0:32, :]
        for r in range(1, 16):
            total = total + received[r * 32:(r + 1) * 32, :]
        for k in range(2):
            for h in range(2):
                where = index[k * 32:(k + 1) * 32, h * 128:(h + 1) * 128]
                value = lanes(total, jnp.maximum(where, 0))
                spread = (first, second)[h]
                spread[pl.ds(k, 32, stride=2), :] = jnp.where(where >= 0, value, 0.0)

    pair = split(jnp.concatenate([first[...], second[...]], axis=1))
    out[...] = dot3(pair, (kh[...], kl[...])).astype(BF16)


def vmem(n):
    return [pl.BlockSpec(memory_space=pltpu.VMEM)] * n


def sds(shape, dtype=F32):
    return jax.ShapeDtypeStruct(shape, dtype)


def call(kernel, shapes, *args, scalars=0, limit=40):
    scalar = [pl.BlockSpec(memory_space=pltpu.SMEM)] * scalars
    many = isinstance(shapes, tuple)
    return pl.pallas_call(
        kernel,
        out_shape=shapes,
        in_specs=scalar + vmem(len(args) - scalars),
        out_specs=tuple(vmem(len(shapes))) if many else vmem(1)[0],
        compiler_params=pltpu.CompilerParams(vmem_limit_bytes=limit << 20),
        name=kernel.__name__,
    )(*args)


def whole(shape):
    return pl.BlockSpec(shape, lambda t: (0,) * len(shape))


def final(turned, grads, momentum, coef, mask, *basis):
    steps = 8
    size = TOKENS // steps
    return pl.pallas_call(
        final_kernel,
        grid=(steps,),
        out_shape=(sds((ROWS, WIDTH)), sds((8, 128))),
        in_specs=[
            pl.BlockSpec((ROWS, size), lambda t: (0, t)),
            pl.BlockSpec((size, WIDTH), lambda t: (t, 0)),
            whole((ROWS, WIDTH)), whole((64, 256)), whole((64, 256)),
            whole((64, 256)), whole((64, 256)), whole((256, 64)), whole((256, 64)),
        ],
        out_specs=(whole((ROWS, WIDTH)), whole((8, 128))),
        compiler_params=pltpu.CompilerParams(vmem_limit_bytes=56 << 20),
        cost_estimate=pl.CostEstimate(flops=2 * TOKENS * ROWS * WIDTH, bytes_accessed=14 << 20, transcendentals=0),
        name="final",
    )(turned, grads, momentum, coef, mask, *basis)


def decode(received, index, done):
    kh, kl = split_np(pair_basis())
    size = 1024
    return pl.pallas_call(
        decode_kernel,
        grid=(CH * CH // size,),
        out_shape=sds((64, CH * CH), BF16),
        in_specs=[
            whole((512, 128)), whole((64, 256)),
            pl.BlockSpec((256, size), lambda t: (0, t)), pl.BlockSpec((256, size), lambda t: (0, t)),
            pl.BlockSpec(memory_space=pl.ANY),
        ],
        out_specs=pl.BlockSpec((64, size), lambda t: (0, t)),
        scratch_shapes=[pltpu.VMEM((64, 128), F32)] * 2,
        compiler_params=pltpu.CompilerParams(vmem_limit_bytes=56 << 20),
        name="decode",
    )(received, index, kh, kl, done)


def shard(z, x, c):
    return (z * 4 + x) * 2 + c


ALONG_X = [[shard(z, x, c) for x in range(4)] for z in range(4) for c in range(2)]
ALONG_Z = [[shard(z, x, c) for z in range(4)] for x in range(4) for c in range(2)]
OTHER_CORE = [(i, i ^ 1) for i in range(32)]


def exchange(copies, groups):
    return lax.all_to_all(copies, "shard", 0, 0, tiled=True, axis_index_groups=groups)


def body(activations, key_grads, momentum, freq_rows, freq_cols, dispatch):
    place = lax.axis_index("shard").astype(I32).reshape(1)
    lh, ll = split_np(block_basis())
    th, tl = lh.T.copy(), ll.T.copy()
    all_grads = lax.all_gather(key_grads, "shard", axis=0, tiled=True)

    band = call(project_kernel, sds((4 * SENT, 256), jnp.int16), key_grads, th, tl)
    along_z = exchange(band, ALONG_Z)
    mask, col_index, row_pick, slot_row, slot_lane, index = call(
        tables_kernel,
        (sds((64, 256)), sds((8, 128), I32), sds((32, 128), I32), sds((32, 128), I32), sds((32, 128), I32),
         sds((64, 256), I32)),
        place, jnp.transpose(freq_rows, (1, 2, 0)), jnp.transpose(freq_cols, (1, 2, 0)), dispatch, scalars=1,
    )
    along_z, slot_row, after = lax.optimization_barrier((along_z, slot_row, jnp.asarray(lh)))
    own = exchange(jnp.broadcast_to(along_z[None], (4, 4 * SENT, 256)).reshape(16 * SENT, 256), ALONG_X)
    high, low, kept, turned = call(
        prepare_kernel,
        (sds((2, 64, 2048), BF16), sds((2, 64, 2048), BF16), sds((64, 256)), sds((ROWS, TOKENS), BF16)),
        activations, momentum, after, ll, th, tl,
    )
    own, kept = lax.optimization_barrier((own, kept))

    other = lax.ppermute(own, "shard", OTHER_CORE)
    near = call(near_kernel, sds((64, 256)), place, high, low, own, kept, scalars=1)
    coef, board = call(
        far_kernel, (sds((64, 256)), sds((512, 128))),
        place, high, low, other, near, col_index, row_pick, slot_row, slot_lane, scalars=1,
    )
    received = lax.all_to_all(board, ("rep", "shard"), 0, 0, tiled=True)
    new_momentum, done = final(turned, all_grads, momentum, coef, mask, lh, ll, th, tl)
    received, done = lax.optimization_barrier((received, done))
    update = decode(received, index, done)
    return (new_momentum, update)


def solution(mesh):
    in_specs = (
        P("rep", "shard"),
        P(("rep", "shard"), None),
        P(("rep", "shard"), None),
        P(),
        P(),
        P(),
    )
    out_specs = (P(("rep", "shard"), None), P("shard", None))
    return jax.shard_map(body, mesh=mesh, in_specs=in_specs, out_specs=out_specs, check_vma=False)
```

time: 141 us -> 127 us (0.901)
  waiting for transfers between devices: 85.2 us -> 42.8 us
  starting transfers between devices: 14.8 us -> 35.9 us
  Pallas kernels: 4.5 us -> 20.7 us
  matrix products: 5.73 us -> 0 us
  local copies, waits for them, and re-layouts: 15.4 us -> 12.3 us
    all_gather x1, waiting for transfers between devices: 68.2 us -> 15.4 us  [body(): all_grads = lax.all_gather(key_grads, 'shard', axis=0, tiled=True)]
    all_to_all x0 -> x2, waiting for transfers between devices: none -> 24.9 us  [exchange(): lax.all_to_all(copies, 'shard', 0, 0, tiled=True, axis_index_groups=groups)]
    all_to_all x1, waiting for transfers between devices: 16.3 us -> 0.01 us  [body(): received = lax.all_to_all(board, ('rep', 'shard'), 0, 0, tiled=True)]
    pallas_call x2 -> x7, Pallas kernels: 4.5 us -> 20.7 us  [the longest x1 9.99 us: final(): pl.pallas_call(final_kernel, grid=(steps,), out_shape=(sds((ROWS, WIDTH))...]
    all_to_all x0 -> x2, starting transfers between devices: none -> 13.9 us  [exchange(): lax.all_to_all(copies, 'shard', 0, 0, tiled=True, axis_index_groups=groups)]
    dot_general x1 -> x0, matrix products: 5.73 us -> none  [body(): lax.dot_general(activations, lax.all_gather(key_grads, 'shard', axis=0, t...]
    ppermute x0 -> x1, starting transfers between devices: none -> 5.21 us  [body(): other = lax.ppermute(own, 'shard', OTHER_CORE)]
    gather x2 -> x0, local copies, waits for them, and re-layouts: 3.64 us -> none  [the longest x1 1.82 us: body(): own_cols = freq_cols.reshape(-1, K)[span_ids].reshape(32, 2, K)]
  transfers between devices with their start and end apart: 2 -> 5, of which waited for: 2 -> 4; matrix products, arithmetic and copies ran while one was open for 9% -> 1% of each run, Pallas kernels for 0% -> 13%
where the time goes in v3:
time: 127 us; the launch traced here: 126 us
  waiting for transfers between devices  42.8 us (34%)
  starting transfers between devices  35.9 us (28%)
  Pallas kernels  20.7 us (16%)
  between operations  14.2 us (11%)
  local copies, waits for them, and re-layouts  12.3 us (10%)
    all_to_all x2, waiting for transfers between devices, exchange(): lax.all_to_all(copies, 'shard', 0, 0, tiled=True, axis_index_groups=groups)  24.9 us
    all_to_all x1, starting transfers between devices, body(): received = lax.all_to_all(board, ('rep', 'shard'), 0, 0, tiled=True)  16.7 us
    all_gather x1, waiting for transfers between devices, body(): all_grads = lax.all_gather(key_grads, 'shard', axis=0, tiled=True)  15.4 us
    all_to_all x2, starting transfers between devices, exchange(): lax.all_to_all(copies, 'shard', 0, 0, tiled=True, axis_index_groups=groups)  13.9 us
    unnamed x46, local copies, waits for them, and re-layouts  11.3 us
    pallas_call x1, Pallas kernels, final(): pl.pallas_call(final_kernel, grid=(steps,), out_shape=(sds((ROWS, WIDTH))...  9.99 us
    pallas_call x5, Pallas kernels, call(): pl.pallas_call(kernel, out_shape=shapes, in_specs=scalar + vmem(len(args)...  5.88 us
    ppermute x1, starting transfers between devices, body(): other = lax.ppermute(own, 'shard', OTHER_CORE)  5.21 us
  transfers between devices with their start and end apart: 5, of which 4 were waited for; matrix products, arithmetic and copies ran while one was open for 1% of the time, Pallas kernels for 13%

profile of v3, /device:TPU:1, one launch (start us, length us, event | category | flops | bytes accessed | tf_op | source)
XLA Modules:
  0.0 125.8 jit_solution(6279610780693531889)
XLA Ops:
  7.9 0.9 copy-done.3
  8.9 0.8 copy-done.4
  9.7 0.8 copy-done.6
  10.5 1.2 project_kernel.1
  11.7 7.8 %all-to-all-start = ((s16[4,144,256]{2,1,0:T(8,128)(2,1)}), s16[4,144,256]{2,1,0:T(8,128)(2,1)S(1)}, u32[]{:S(2)}, u32[]{:S(2)}) async-start(s16[4,144,256]{2,1,0:T(8,128)(2,1)} %bitcast), calls=%async_computation | async-start | bytes 589824 | tf_op jit(solution)/shard_map/all_to_all | solution.py:320
  19.6 0.9 copy-done.13
  20.5 0.8 copy-done.14
  21.4 0.7 copy-done.19
  22.1 0.7 tables_kernel.1
  24.6 0.9 all-to-all-done
  25.5 1.1 broadcast_in_dim.2
  26.6 6.1 %all-to-all-start.1 = ((s16[4,576,256]{2,1,0:T(8,128)(2,1)}), s16[4,576,256]{2,1,0:T(8,128)(2,1)S(1)}, u32[]{:S(2)}, u32[]{:S(2)}) async-start(s16[4,576,256]{2,1,0:T(8,128)(2,1)} %broadcast_in_dim.2), calls=%async_computation.1 | async-start | bytes 2359296 | tf_op jit(solution)/shard_map/all_to_all | solution.py:320
  32.7 1.6 %copy-done.1 = bf16[4096,256]{1,0:T(8,128)(2,1)S(1)} copy-done((bf16[4096,256]{1,0:T(8,128)(2,1)S(1)}, bf16[4096,256]{1,0:T(8,128)(2,1)}, u32[]{:S(2)}) %copy-start.1) | copy-done | bytes 2097176
  34.4 1.5 %prepare_kernel.1 = (bf16[2,64,2048]{2,1,0:T(8,128)(2,1)S(1)}, bf16[2,64,2048]{2,1,0:T(8,128)(2,1)S(1)}, f32[64,256]{1,0:T(8,128)S(1)}, bf16[256,4096]{1,0:T(8,128)(2,1)S(1)}) custom-call(bf16[4096,256]{1,0:T(8,128)(2,1)S(1)} %copy-done.1, f32[256,1024]{1,0:T(8,128)S(1)} %copy-done, bf16[64,256]{1,0:T(8,128)(2,1)S(1)} %copy-done.8, ...), custom_call_target="tpu_custom_call" | custom-call | tf_op jit(solution)/shard_map/prepare_kernel/pallas_call | solution.py:257
  35.8 1.4 %copy-done.2 = bf16[256,4096]{1,0:T(8,128)(2,1)} copy-done((bf16[256,4096]{1,0:T(8,128)(2,1)}, bf16[256,4096]{1,0:T(8,128)(2,1)S(1)}, u32[]{:S(2)}) %copy-start.2) | copy-done | bytes 2097176
  37.2 24.0 %all-to-all-done.1 = s16[4,576,256]{2,1,0:T(8,128)(2,1)S(1)} async-done(((s16[4,576,256]{2,1,0:T(8,128)(2,1)}), s16[4,576,256]{2,1,0:T(8,128)(2,1)S(1)}, u32[]{:S(2)}, u32[]{:S(2)}) %all-to-all-start.1) | async-done | bytes 1179680 | tf_op jit(solution)/shard_map/all_to_all | solution.py:320
  61.3 5.2 %collective-permute-start = (s16[2304,256]{1,0:T(8,128)(2,1)S(1)}, s16[2304,256]{1,0:T(8,128)(2,1)S(1)}, u32[]{:S(2)}, u32[]{:S(2)}) collective-permute-start(s16[2304,256]{1,0:T(8,128)(2,1)S(1)} %bitcast.10), channel_id=1, source_target_pairs={{0,1},{1,0},{2,3},{3,2},{4,5},{5,4},{6,7},{7,6},{8,9},{9,8},{10,11... | collective-permute-start | bytes 3538952 | tf_op jit(solution)/shard_map/ppermute | solution.py:346
  67.1 1.8 %collective-permute-done.other = s16[2304,256]{1,0:T(8,128)(2,1)S(1)} collective-permute-done((s16[2304,256]{1,0:T(8,128)(2,1)S(1)}, s16[2304,256]{1,0:T(8,128)(2,1)S(1)}, u32[]{:S(2)}, u32[]{:S(2)}) %collective-permute-start) | collective-permute-done | bytes 1179680 | tf_op jit(solution)/shard_map/ppermute | solution.py:346
  69.0 1.9 %far_kernel.1 = (f32[64,256]{1,0:T(8,128)S(1)}, f32[512,128]{1,0:T(8,128)}) custom-call(s32[1]{0:T(128)} %bitcast.2.place, bf16[2,64,2048]{2,1,0:T(8,128)(2,1)S(1)} %get-tuple-element.26.high, bf16[2,64,2048]{2,1,0:T(8,128)(2,1)S(1)} %get-tuple-element.27.low, s16[2304,256]{1,0:T(8,128)(2,1)S(1)} %collective-permute-done.other, ...), custom_call_target="tpu_custom_call" | custom-call | tf_op jit(solution)/shard_map/far_kernel/pallas_call | solution.py:257
  71.5 16.7 %all-to-all-start.2 = ((f32[512,1,128]{2,1,0:T(1,128)}), f32[512,1,128]{2,1,0:T(1,128)S(1)}, u32[]{:S(2)}, u32[]{:S(2)}) async-start(f32[512,1,128]{2,1,0:T(1,128)} %bitcast.7), calls=%async_computation.2 | async-start | bytes 524288 | tf_op jit(solution)/shard_map/all_to_all | solution.py:352
  88.2 15.4 %all-gather.2.cloned.1.call-done.grads = bf16[4096,1024]{1,0:T(8,128)(2,1)} async-done(((bf16[128,1024]{1,0:T(8,128)(2,1)}), bf16[4096,1024]{1,0:T(8,128)(2,1)}) %all-gather.2.cloned.1.call-update) | async-done | bytes 8388624 | tf_op jit(solution)/shard_map/all_gather | solution.py:327
  103.5 10.0 %final.1 = (f32[256,1024]{1,0:T(8,128)}, f32[8,128]{1,0:T(8,128)}) custom-call(bf16[256,4096]{1,0:T(8,128)(2,1)} %copy-done.2, bf16[4096,1024]{1,0:T(8,128)(2,1)} %all-gather.2.cloned.1.call-done.grads, f32[256,1024]{1,0:T(8,128)} %momentum.3, f32[64,256]{1,0:T(8,128)} %copy-done.12, f32[64,256]{1,0:T(8,128)} %copy-done.11, ...), custom_call_target="tpu_custom_call" | custom-call | flops 2147483648 | bytes 14680064 | tf_op jit(solution)/shard_map/final/pallas_call | solution.py:274
  113.5 0.7 copy-done.22
  114.2 4.8 %decode.1 = bf16[64,4096]{1,0:T(8,128)(2,1)} custom-call(f32[512,128]{1,0:T(8,128)} %bitcast.15, s32[64,256]{1,0:T(8,128)} %copy-done.10, bf16[256,4096]{1,0:T(8,128)(2,1)} %constant.20.clone.kh, bf16[256,4096]{1,0:T(8,128)(2,1)} %constant.21.clone.kl, f32[8,128]{1,0:T(8,128)} %get-tuple-element.43.done), custom_call_target="tpu_custom_call" | custom-call | tf_op jit(solution)/shard_map/decode/pallas_call | solution.py:294
  (41 shorter events, 3.9 us)
Async XLA Ops:
  7.2 96.3 %all-gather.2.cloned.1.call-start = ((), (), s32[]{:S(2)}) async-start(), calls=%async_computation.3 | async-start | bytes 8650752 | tf_op jit(solution)/shard_map/all_gather | solution.py:327
  7.9 1.0 copy-start.3
  8.8 0.8 copy-start.4
  9.7 0.8 copy-start.6
  11.7 13.7 %all-to-all-start = ((s16[4,144,256]{2,1,0:T(8,128)(2,1)}), s16[4,144,256]{2,1,0:T(8,128)(2,1)S(1)}, u32[]{:S(2)}, u32[]{:S(2)}) async-start(s16[4,144,256]{2,1,0:T(8,128)(2,1)} %bitcast), calls=%async_computation | async-start | bytes 589824 | tf_op jit(solution)/shard_map/all_to_all | solution.py:320
  19.5 13.2 %copy-start = (f32[256,1024]{1,0:T(8,128)S(1)}, f32[256,1024]{1,0:T(8,128)}, u32[]{:S(2)}) copy-start(f32[256,1024]{1,0:T(8,128)} %momentum.3) | copy-start | bytes 3145732
  19.5 13.2 %copy-start.5 = (bf16[256,64]{1,0:T(8,128)(2,1)S(1)}, bf16[256,64]{1,0:T(8,128)(2,1)}, u32[]{:S(2)}) copy-start(bf16[256,64]{1,0:T(8,128)(2,1)} %constant.16.clone.th) | copy-start | bytes 98308
  19.5 13.2 %copy-start.7 = (bf16[256,64]{1,0:T(8,128)(2,1)S(1)}, bf16[256,64]{1,0:T(8,128)(2,1)}, u32[]{:S(2)}) copy-start(bf16[256,64]{1,0:T(8,128)(2,1)} %constant.17.clone.tl) | copy-start | bytes 98308
  19.5 13.2 %copy-start.8 = (bf16[64,256]{1,0:T(8,128)(2,1)S(1)}, bf16[64,256]{1,0:T(8,128)(2,1)}, u32[]{:S(2)}) copy-start(bf16[64,256]{1,0:T(8,128)(2,1)} %constant.18.clone.lh) | copy-start | bytes 98308
  19.6 13.2 %copy-start.9 = (bf16[64,256]{1,0:T(8,128)(2,1)S(1)}, bf16[64,256]{1,0:T(8,128)(2,1)}, u32[]{:S(2)}) copy-start(bf16[64,256]{1,0:T(8,128)(2,1)} %constant.19.clone.ll) | copy-start | bytes 98308
  19.6 0.9 copy-start.13
  20.5 0.8 copy-start.14
  21.4 0.7 copy-start.19
  24.6 2.0 %copy-start.10 = (s32[64,256]{1,0:T(8,128)}, s32[64,256]{1,0:T(8,128)S(1)}, u32[]{:S(2)}) copy-start(s32[64,256]{1,0:T(8,128)S(1)} %get-tuple-element.42.index) | copy-start | bytes 196612
  24.6 2.0 %copy-start.17 = (s32[32,128]{1,0:T(8,128)}, s32[32,128]{1,0:T(8,128)S(1)}, u32[]{:S(2)}) copy-start(s32[32,128]{1,0:T(8,128)S(1)} %get-tuple-element.35.slot_lane) | copy-start | bytes 49156
  26.6 34.7 %all-to-all-start.1 = ((s16[4,576,256]{2,1,0:T(8,128)(2,1)}), s16[4,576,256]{2,1,0:T(8,128)(2,1)S(1)}, u32[]{:S(2)}, u32[]{:S(2)}) async-start(s16[4,576,256]{2,1,0:T(8,128)(2,1)} %broadcast_in_dim.2), calls=%async_computation.1 | async-start | bytes 2359296 | tf_op jit(solution)/shard_map/all_to_all | solution.py:320
  32.7 1.6 %copy-start.1 = (bf16[4096,256]{1,0:T(8,128)(2,1)S(1)}, bf16[4096,256]{1,0:T(8,128)(2,1)}, u32[]{:S(2)}) copy-start(bf16[4096,256]{1,0:T(8,128)(2,1)} %inputs.1) | copy-start | bytes 6291460
  35.8 1.4 %copy-start.2 = (bf16[256,4096]{1,0:T(8,128)(2,1)}, bf16[256,4096]{1,0:T(8,128)(2,1)S(1)}, u32[]{:S(2)}) copy-start(bf16[256,4096]{1,0:T(8,128)(2,1)S(1)} %get-tuple-element.25.turned) | copy-start | bytes 6291460
  37.2 31.8 %copy-start.16 = (s32[32,128]{1,0:T(8,128)S(1)}, s32[32,128]{1,0:T(8,128)}, u32[]{:S(2)}) copy-start(s32[32,128]{1,0:T(8,128)} %copy-done.15) | copy-start | bytes 49156
  37.2 31.8 %copy-start.18 = (s32[32,128]{1,0:T(8,128)S(1)}, s32[32,128]{1,0:T(8,128)}, u32[]{:S(2)}) copy-start(s32[32,128]{1,0:T(8,128)} %copy-done.17) | copy-start | bytes 49156
  37.2 31.8 %copy-start.21 = (s32[8,128]{1,0:T(8,128)S(1)}, s32[8,128]{1,0:T(8,128)}, u32[]{:S(2)}) copy-start(s32[8,128]{1,0:T(8,128)} %copy-done.20) | copy-start | bytes 12292
  61.3 7.7 %collective-permute-start = (s16[2304,256]{1,0:T(8,128)(2,1)S(1)}, s16[2304,256]{1,0:T(8,128)(2,1)S(1)}, u32[]{:S(2)}, u32[]{:S(2)}) collective-permute-start(s16[2304,256]{1,0:T(8,128)(2,1)S(1)} %bitcast.10), channel_id=1, source_target_pairs={{0,1},{1,0},{2,3},{3,2},{4,5},{5,4},{6,7},{7,6},{8,9},{9,8},{10,11... | collective-permute-start | bytes 3538952 | tf_op jit(solution)/shard_map/ppermute | solution.py:346
  71.5 42.0 %all-to-all-start.2 = ((f32[512,1,128]{2,1,0:T(1,128)}), f32[512,1,128]{2,1,0:T(1,128)S(1)}, u32[]{:S(2)}, u32[]{:S(2)}) async-start(f32[512,1,128]{2,1,0:T(1,128)} %bitcast.7), calls=%async_computation.2 | async-start | bytes 524288 | tf_op jit(solution)/shard_map/all_to_all | solution.py:352
  113.5 0.7 copy-start.22
  (4 other events, 2.4 us)
Sparse Core Ops, SparseCore 0:
  10.1 93.3 all-gather.1

commit v4 on v3

--- a/solution.py
+++ b/solution.py
@@ -12,6 +12,7 @@
 ROWS = 256
 WIDTH = 1024
 TOKENS = 4096
+STEPS = 8
 LEVELS = 32000.0
 SENT = 144
 F32 = jnp.float32
@@ -34,10 +35,6 @@
 
 def block_basis():
     return np.kron(np.eye(4), band_table())
-
-
-def pair_basis():
-    return np.kron(band_table(), band_table())
 
 
 def split(x):
@@ -148,7 +145,7 @@
         index[:, h * 128:(h + 1) * 128] = jnp.where(row_seen * col_seen > 0, found, -1)
 
 
-def prepare_kernel(inputs, momentum, lh, ll, th, tl, high, low, kept, turned):
+def prepare_kernel(inputs, momentum, lh, ll, th, tl, high, low, kept):
     both_basis = jnp.concatenate([lh[...], ll[...]], axis=0)
     for z in range(4):
         for x in range(4):
@@ -160,7 +157,6 @@
                 to = (x * 4 + z) * 128
                 high[c, :, to:to + 128] = part[0]
                 low[c, :, to:to + 128] = part[1]
-                turned[:, at:at + 128] = block.T
     left, right = (lh[...], ll[...]), (th[...], tl[...])
     half = dot3(left, split(0.999 * momentum[...]))
     for q in range(4):
@@ -213,34 +209,69 @@
         sent[r * 32:(r + 1) * 32, :] = board
 
 
-def final_kernel(turned, grads, momentum, coef, mask, lh, ll, th, tl, out, done):
-    @pl.when(pl.program_id(0) == 0)
-    def _():
-        left, right = (lh[...], ll[...]), (th[...], tl[...])
-        back = dot3(right, split(coef[...] * mask[...]))
+def ready_kernel(inputs, momentum, coef, mask, lh, ll, th, tl, turned, base):
+    size = TOKENS // STEPS
+    for k in range(STEPS):
+        turned[k] = inputs[k * size:(k + 1) * size, :].T
+    left, right = (lh[...], ll[...]), (th[...], tl[...])
+    back = dot3(right, split(coef[...] * mask[...]))
+    for q in range(4):
+        cols = slice(q * 256, (q + 1) * 256)
+        base[:, cols] = 0.999 * momentum[:, cols] - dot3(split(back[:, q * 64:(q + 1) * 64]), left)
+
+
+def final_kernel(turned, grads, base, out, done, sides, held, start, sems):
+    size = TOKENS // STEPS
+    first = pltpu.make_async_copy(base, start, sems.at[2 * STEPS])
+    copies = []
+    for k in range(STEPS):
+        rows = pl.ds(k * size, size)
+        copies.append((
+            pltpu.make_async_copy(turned.at[k], sides.at[k], sems.at[STEPS + k]),
+            pltpu.make_async_copy(grads.at[rows], held.at[rows], sems.at[k]),
+        ))
+        for copy in copies[k]:
+            copy.start()
+        if k == 0:
+            first.start()
+    done[...] = jnp.zeros((8, 128), F32)
+    for k in range(STEPS):
+        for copy in copies[k]:
+            copy.wait()
+        if k == 0:
+            first.wait()
+        rows = slice(k * size, (k + 1) * size)
         for q in range(4):
             cols = slice(q * 256, (q + 1) * 256)
-            out[:, cols] = 0.999 * momentum[:, cols] - dot3(split(back[:, q * 64:(q + 1) * 64]), left)
-        done[...] = jnp.zeros((8, 128), F32)
-
-    out[...] += dot(turned[...], grads[...])
-
-
-def decode_kernel(received, index, kh, kl, done, out, first, second):
-    @pl.when(pl.program_id(0) == 0)
-    def _():
-        total = received[0:32, :]
-        for r in range(1, 16):
-            total = total + received[r * 32:(r + 1) * 32, :]
-        for k in range(2):
-            for h in range(2):
-                where = index[k * 32:(k + 1) * 32, h * 128:(h + 1) * 128]
-                value = lanes(total, jnp.maximum(where, 0))
-                spread = (first, second)[h]
-                spread[pl.ds(k, 32, stride=2), :] = jnp.where(where >= 0, value, 0.0)
-
-    pair = split(jnp.concatenate([first[...], second[...]], axis=1))
-    out[...] = dot3(pair, (kh[...], kl[...])).astype(BF16)
+            out[:, cols] = (start if k == 0 else out)[:, cols] + dot(sides[k], held[rows, cols])
+
+
+def decode_kernel(received, index, weights, lh, ll, done, out, first, second, wide):
+    total = received[0:32, :]
+    for r in range(1, 16):
+        total = total + received[r * 32:(r + 1) * 32, :]
+    for k in range(2):
+        for h in range(2):
+            where = index[k * 32:(k + 1) * 32, h * 128:(h + 1) * 128]
+            value = lanes(total, jnp.maximum(where, 0))
+            spread = (first, second)[h]
+            spread[pl.ds(k, 32, stride=2), :] = jnp.where(where >= 0, value, 0.0)
+    basis = (lh[...], ll[...])
+    for q in range(4):
+        part = (first, second)[q // 2][:, (q % 2) * 64:(q % 2) * 64 + 64]
+        columns = dot3(split(part), basis)
+        for f in range(4):
+            piece = columns[:, f * 64:(f + 1) * 64]
+            wide[q * 4 + f] = jnp.concatenate([piece, piece], axis=1)
+
+    @pl.loop(0, CH // 2)
+    def _(pair):
+        row = pl.multiple_of(pair * BAND, BAND)
+        factors = weights[pl.ds(row, BAND), :]
+        value = wide[0] * factors[0:1]
+        for f in range(1, BAND):
+            value = value + wide[f] * factors[f:f + 1]
+        out[:, pl.ds(pl.multiple_of(pair * 128, 128), 128)] = value.astype(BF16)
 
 
 def vmem(n):
@@ -264,47 +295,34 @@
     )(*args)
 
 
-def whole(shape):
-    return pl.BlockSpec(shape, lambda t: (0,) * len(shape))
-
-
-def final(turned, grads, momentum, coef, mask, *basis):
-    steps = 8
-    size = TOKENS // steps
+def final(turned, grads, base):
     return pl.pallas_call(
         final_kernel,
-        grid=(steps,),
         out_shape=(sds((ROWS, WIDTH)), sds((8, 128))),
-        in_specs=[
-            pl.BlockSpec((ROWS, size), lambda t: (0, t)),
-            pl.BlockSpec((size, WIDTH), lambda t: (t, 0)),
-            whole((ROWS, WIDTH)), whole((64, 256)), whole((64, 256)),
-            whole((64, 256)), whole((64, 256)), whole((256, 64)), whole((256, 64)),
+        in_specs=[pl.BlockSpec(memory_space=pl.ANY)] * 3,
+        out_specs=tuple(vmem(2)),
+        scratch_shapes=[
+            pltpu.VMEM((STEPS, ROWS, TOKENS // STEPS), BF16), pltpu.VMEM((TOKENS, WIDTH), BF16),
+            pltpu.VMEM((ROWS, WIDTH), F32), pltpu.SemaphoreType.DMA((2 * STEPS + 1,)),
         ],
-        out_specs=(whole((ROWS, WIDTH)), whole((8, 128))),
         compiler_params=pltpu.CompilerParams(vmem_limit_bytes=56 << 20),
         cost_estimate=pl.CostEstimate(flops=2 * TOKENS * ROWS * WIDTH, bytes_accessed=14 << 20, transcendentals=0),
         name="final",
-    )(turned, grads, momentum, coef, mask, *basis)
-
-
-def decode(received, index, done):
-    kh, kl = split_np(pair_basis())
-    size = 1024
+    )(turned, grads, base)
+
+
+def decode(received, index, lh, ll, done):
+    table = band_table().T.reshape(CH // 2, 2, BAND).transpose(0, 2, 1)
+    weights = np.repeat(table, 64, axis=2).reshape(CH // 2 * BAND, 128).astype(np.float32)
     return pl.pallas_call(
         decode_kernel,
-        grid=(CH * CH // size,),
         out_shape=sds((64, CH * CH), BF16),
-        in_specs=[
-            whole((512, 128)), whole((64, 256)),
-            pl.BlockSpec((256, size), lambda t: (0, t)), pl.BlockSpec((256, size), lambda t: (0, t)),
-            pl.BlockSpec(memory_space=pl.ANY),
-        ],
-        out_specs=pl.BlockSpec((64, size), lambda t: (0, t)),
-        scratch_shapes=[pltpu.VMEM((64, 128), F32)] * 2,
-        compiler_params=pltpu.CompilerParams(vmem_limit_bytes=56 << 20),
+        in_specs=vmem(5) + [pl.BlockSpec(memory_space=pl.ANY)],
+        out_specs=vmem(1)[0],
+        scratch_shapes=[pltpu.VMEM((64, 128), F32)] * 2 + [pltpu.VMEM((BAND, 64, 128), F32)],
+        compiler_params=pltpu.CompilerParams(vmem_limit_bytes=24 << 20),
         name="decode",
-    )(received, index, kh, kl, done)
+    )(received, index, weights, lh, ll, done)
 
 
 def shard(z, x, c):
@@ -326,7 +344,7 @@
     th, tl = lh.T.copy(), ll.T.copy()
     all_grads = lax.all_gather(key_grads, "shard", axis=0, tiled=True)
 
-    band = call(project_kernel, sds((4 * SENT, 256), jnp.int16), key_grads, th, tl)
+    band = call(project_kernel, sds((4 * SENT, 256), jnp.int16), key_grads, th, tl, limit=56)
     along_z = exchange(band, ALONG_Z)
     mask, col_index, row_pick, slot_row, slot_lane, index = call(
         tables_kernel,
@@ -336,9 +354,9 @@
     )
     along_z, slot_row, after = lax.optimization_barrier((along_z, slot_row, jnp.asarray(lh)))
     own = exchange(jnp.broadcast_to(along_z[None], (4, 4 * SENT, 256)).reshape(16 * SENT, 256), ALONG_X)
-    high, low, kept, turned = call(
+    high, low, kept = call(
         prepare_kernel,
-        (sds((2, 64, 2048), BF16), sds((2, 64, 2048), BF16), sds((64, 256)), sds((ROWS, TOKENS), BF16)),
+        (sds((2, 64, 2048), BF16), sds((2, 64, 2048), BF16), sds((64, 256))),
         activations, momentum, after, ll, th, tl,
     )
     own, kept = lax.optimization_barrier((own, kept))
@@ -350,9 +368,13 @@
         place, high, low, other, near, col_index, row_pick, slot_row, slot_lane, scalars=1,
     )
     received = lax.all_to_all(board, ("rep", "shard"), 0, 0, tiled=True)
-    new_momentum, done = final(turned, all_grads, momentum, coef, mask, lh, ll, th, tl)
+    turned, base = call(
+        ready_kernel, (sds((STEPS, ROWS, TOKENS // STEPS), BF16), sds((ROWS, WIDTH))),
+        activations, momentum, coef, mask, lh, ll, th, tl,
+    )
+    new_momentum, done = final(turned, all_grads, base)
     received, done = lax.optimization_barrier((received, done))
-    update = decode(received, index, done)
+    update = decode(received, index, lh, ll, done)
     return (new_momentum, update)
 
 

time: 127 us -> 120 us (0.945)
  waiting for transfers between devices: 42.8 us -> 36 us
  local copies, waits for them, and re-layouts: 12.3 us -> 16.9 us
  Pallas kernels: 20.7 us -> 16.4 us
    pallas_call x2, Pallas kernels: 14.8 us -> 8.69 us  [the longest x1 5.9 us: final(): pl.pallas_call(final_kernel, out_shape=(sds((ROWS, WIDTH)), sds((8, 128))...]
    unnamed x46 -> x56, local copies, waits for them, and re-layouts: 11.3 us -> 15.8 us
    all_gather x1, waiting for transfers between devices: 15.4 us -> 10.9 us  [body(): all_grads = lax.all_gather(key_grads, 'shard', axis=0, tiled=True)]
    ppermute x1, waiting for transfers between devices: 1.83 us -> 0.01 us  [body(): other = lax.ppermute(own, 'shard', OTHER_CORE)]
    pallas_call x5 -> x6, Pallas kernels: 5.88 us -> 7.68 us  [call(): pl.pallas_call(kernel, out_shape=shapes, in_specs=scalar + vmem(len(args)...]
  transfers between devices with their start and end apart: 5 -> 5, of which waited for: 4 -> 3; matrix products, arithmetic and copies ran while one was open for 1% -> 1% of each run, Pallas kernels for 13% -> 11%
where the time goes in v4:
time: 120 us; the launch traced here: 119 us
  waiting for transfers between devices  36 us (30%)
  starting transfers between devices  35.6 us (30%)
  local copies, waits for them, and re-layouts  16.9 us (14%)
  Pallas kernels  16.4 us (14%)
  between operations  14.2 us (12%)
    all_to_all x2, waiting for transfers between devices, exchange(): lax.all_to_all(copies, 'shard', 0, 0, tiled=True, axis_index_groups=groups)  24.4 us
    all_to_all x1, starting transfers between devices, body(): received = lax.all_to_all(board, ('rep', 'shard'), 0, 0, tiled=True)  16 us
    unnamed x56, local copies, waits for them, and re-layouts  15.8 us
    all_to_all x2, starting transfers between devices, exchange(): lax.all_to_all(copies, 'shard', 0, 0, tiled=True, axis_index_groups=groups)  13.9 us
    all_gather x1, waiting for transfers between devices, body(): all_grads = lax.all_gather(key_grads, 'shard', axis=0, tiled=True)  10.9 us
    pallas_call x6, Pallas kernels, call(): pl.pallas_call(kernel, out_shape=shapes, in_specs=scalar + vmem(len(args)...  7.68 us
    pallas_call x1, Pallas kernels, final(): pl.pallas_call(final_kernel, out_shape=(sds((ROWS, WIDTH)), sds((8, 128))...  5.9 us
    ppermute x1, starting transfers between devices, body(): other = lax.ppermute(own, 'shard', OTHER_CORE)  5.69 us
  transfers between devices with their start and end apart: 5, of which 3 were waited for; matrix products, arithmetic and copies ran while one was open for 1% of the time, Pallas kernels for 11%

profile of v4, /device:TPU:1, one launch (start us, length us, event | category | flops | bytes accessed | tf_op | source)
XLA Modules:
  0.0 119.2 jit_solution(14299194567641029673)
XLA Ops:
  7.9 2.2 %project_kernel.1 = s16[576,256]{1,0:T(8,128)(2,1)} custom-call(bf16[128,1024]{1,0:T(8,128)(2,1)} %grads.1, bf16[256,64]{1,0:T(8,128)(2,1)} %constant.14.clone.th, bf16[256,64]{1,0:T(8,128)(2,1)} %constant.15.clone.tl), custom_call_target="tpu_custom_call" | custom-call | tf_op jit(solution)/shard_map/project_kernel/pallas_call | solution.py:288
  10.1 7.8 %all-to-all-start = ((s16[4,144,256]{2,1,0:T(8,128)(2,1)}), s16[4,144,256]{2,1,0:T(8,128)(2,1)S(1)}, u32[]{:S(2)}, u32[]{:S(2)}) async-start(s16[4,144,256]{2,1,0:T(8,128)(2,1)} %bitcast.16), calls=%async_computation | async-start | bytes 589824 | tf_op jit(solution)/shard_map/all_to_all | solution.py:338
  18.0 1.0 copy-done.18
  19.0 0.8 copy-done.19
  23.0 0.8 all-to-all-done
  23.8 1.1 broadcast_in_dim.2
  25.0 6.1 %all-to-all-start.1 = ((s16[4,576,256]{2,1,0:T(8,128)(2,1)}), s16[4,576,256]{2,1,0:T(8,128)(2,1)S(1)}, u32[]{:S(2)}, u32[]{:S(2)}) async-start(s16[4,576,256]{2,1,0:T(8,128)(2,1)} %broadcast_in_dim.2), calls=%async_computation.1 | async-start | bytes 2359296 | tf_op jit(solution)/shard_map/all_to_all | solution.py:338
  31.1 1.2 %copy-done.1 = f32[256,1024]{1,0:T(8,128)S(1)} copy-done((f32[256,1024]{1,0:T(8,128)S(1)}, f32[256,1024]{1,0:T(8,128)}, u32[]{:S(2)}) %copy-start.1) | copy-done | bytes 1048600
  32.3 1.4 %prepare_kernel.1 = (bf16[2,64,2048]{2,1,0:T(8,128)(2,1)S(1)}, bf16[2,64,2048]{2,1,0:T(8,128)(2,1)S(1)}, f32[64,256]{1,0:T(8,128)S(1)}) custom-call(bf16[4096,256]{1,0:T(8,128)(2,1)S(1)} %copy-done, f32[256,1024]{1,0:T(8,128)S(1)} %copy-done.1, bf16[64,256]{1,0:T(8,128)(2,1)S(1)} %copy-done.11, bf16[64,256]{1,0:T(8,128)(2,1)S(1)} %copy-done.12, ...), custom_call_target="tpu_custom_call" | custom-call | tf_op jit(solution)/shard_map/prepare_kernel/pallas_call | solution.py:288
  35.9 23.6 %all-to-all-done.1 = s16[4,576,256]{2,1,0:T(8,128)(2,1)S(1)} async-done(((s16[4,576,256]{2,1,0:T(8,128)(2,1)}), s16[4,576,256]{2,1,0:T(8,128)(2,1)S(1)}, u32[]{:S(2)}, u32[]{:S(2)}) %all-to-all-start.1) | async-done | bytes 1179680 | tf_op jit(solution)/shard_map/all_to_all | solution.py:338
  59.5 5.7 %collective-permute-start = (s16[2304,256]{1,0:T(8,128)(2,1)S(1)}, s16[2304,256]{1,0:T(8,128)(2,1)S(1)}, u32[]{:S(2)}, u32[]{:S(2)}) collective-permute-start(s16[2304,256]{1,0:T(8,128)(2,1)S(1)} %bitcast.10), channel_id=1, source_target_pairs={{0,1},{1,0},{2,3},{3,2},{4,5},{5,4},{6,7},{7,6},{8,9},{9,8},{10,11... | collective-permute-start | bytes 3538952 | tf_op jit(solution)/shard_map/ppermute | solution.py:364
  65.2 1.0 copy-done.4
  66.2 1.0 copy-done.6
  67.3 0.8 copy-done.17
  68.9 1.9 %far_kernel.1 = (f32[64,256]{1,0:T(8,128)S(1)}, f32[512,128]{1,0:T(8,128)}) custom-call(s32[1]{0:T(128)} %bitcast.place, bf16[2,64,2048]{2,1,0:T(8,128)(2,1)S(1)} %copy-done.4, bf16[2,64,2048]{2,1,0:T(8,128)(2,1)S(1)} %copy-done.6, s16[2304,256]{1,0:T(8,128)(2,1)S(1)} %collective-permute-done.other, f32[64,256]{1,0:T(8,128)S(1)} %near_kernel.1.near, ...), custom_call_target="tpu_custom_call" | custom-call | tf_op jit(solution)/shard_map/far_kernel/pallas_call | solution.py:288
  70.7 16.0 %all-to-all-start.2 = ((f32[512,1,128]{2,1,0:T(1,128)}), f32[512,1,128]{2,1,0:T(1,128)S(1)}, u32[]{:S(2)}, u32[]{:S(2)}) async-start(f32[512,1,128]{2,1,0:T(1,128)} %bitcast.7), calls=%async_computation.2 | async-start | bytes 524288 | tf_op jit(solution)/shard_map/all_to_all | solution.py:370
  86.7 1.2 %copy-done.2 = f32[256,1024]{1,0:T(8,128)S(1)} copy-done((f32[256,1024]{1,0:T(8,128)S(1)}, f32[256,1024]{1,0:T(8,128)}, u32[]{:S(2)}) %copy-start.2) | copy-done | bytes 1048600
  87.9 0.8 copy-done.15
  88.8 0.9 ready_kernel.1
  89.7 1.3 %copy-done.7 = bf16[8,256,512]{2,1,0:T(8,128)(2,1)} copy-done((bf16[8,256,512]{2,1,0:T(8,128)(2,1)}, bf16[8,256,512]{2,1,0:T(8,128)(2,1)S(1)}, u32[]{:S(2)}) %copy-start.7) | copy-done | bytes 2097176
  91.0 1.0 copy-done.8
  92.0 10.9 %all-gather.2.cloned.1.call-done.grads = bf16[4096,1024]{1,0:T(8,128)(2,1)} async-done(((bf16[128,1024]{1,0:T(8,128)(2,1)}), bf16[4096,1024]{1,0:T(8,128)(2,1)}) %all-gather.2.cloned.1.call-update) | async-done | bytes 8388624 | tf_op jit(solution)/shard_map/all_gather | solution.py:345
  102.9 5.9 %final.1 = (f32[256,1024]{1,0:T(8,128)}, f32[8,128]{1,0:T(8,128)}) custom-call(bf16[8,256,512]{2,1,0:T(8,128)(2,1)} %copy-done.7, bf16[4096,1024]{1,0:T(8,128)(2,1)} %all-gather.2.cloned.1.call-done.grads, f32[256,1024]{1,0:T(8,128)} %copy-done.8), custom_call_target="tpu_custom_call" | custom-call | flops 2147483648 | bytes 14680064 | tf_op jit(solution)/shard_map/final/pallas_call | solution.py:299
  109.6 2.8 %decode.1 = bf16[64,4096]{1,0:T(8,128)(2,1)} custom-call(f32[512,128]{1,0:T(8,128)S(1)} %bitcast.12, s32[64,256]{1,0:T(8,128)S(1)} %get-tuple-element.44.index, f32[512,128]{1,0:T(8,128)S(1)} %copy-done.13, bf16[64,256]{1,0:T(8,128)(2,1)S(1)} %copy-done.11, bf16[64,256]{1,0:T(8,128)(2,1)S(1)} %copy-done.12, f32[8,128]{1,0:T(8,128)S(1)} %copy-done.27), custom_call_target="tpu_custom_call" | custom-call | tf_op jit(solution)/shard_map/decode/pallas_call | solution.py:317
  (52 shorter events, 7.6 us)
Async XLA Ops:
  7.2 95.8 %all-gather.2.cloned.1.call-start = ((), (), s32[]{:S(2)}) async-start(), calls=%async_computation.3 | async-start | bytes 8650752 | tf_op jit(solution)/shard_map/all_gather | solution.py:345
  10.1 13.7 %all-to-all-start = ((s16[4,144,256]{2,1,0:T(8,128)(2,1)}), s16[4,144,256]{2,1,0:T(8,128)(2,1)S(1)}, u32[]{:S(2)}, u32[]{:S(2)}) async-start(s16[4,144,256]{2,1,0:T(8,128)(2,1)} %bitcast.16), calls=%async_computation | async-start | bytes 589824 | tf_op jit(solution)/shard_map/all_to_all | solution.py:338
  17.9 13.2 %copy-start = (bf16[4096,256]{1,0:T(8,128)(2,1)S(1)}, bf16[4096,256]{1,0:T(8,128)(2,1)}, u32[]{:S(2)}) copy-start(bf16[4096,256]{1,0:T(8,128)(2,1)} %inputs.3) | copy-start | bytes 6291460
  17.9 13.2 %copy-start.9 = (bf16[256,64]{1,0:T(8,128)(2,1)S(1)}, bf16[256,64]{1,0:T(8,128)(2,1)}, u32[]{:S(2)}) copy-start(bf16[256,64]{1,0:T(8,128)(2,1)} %constant.15.clone.tl) | copy-start | bytes 98308
  17.9 13.2 %copy-start.10 = (bf16[256,64]{1,0:T(8,128)(2,1)S(1)}, bf16[256,64]{1,0:T(8,128)(2,1)}, u32[]{:S(2)}) copy-start(bf16[256,64]{1,0:T(8,128)(2,1)} %constant.14.clone.th) | copy-start | bytes 98308
  17.9 13.2 %copy-start.11 = (bf16[64,256]{1,0:T(8,128)(2,1)S(1)}, bf16[64,256]{1,0:T(8,128)(2,1)}, u32[]{:S(2)}) copy-start(bf16[64,256]{1,0:T(8,128)(2,1)} %constant.16.clone.lh) | copy-start | bytes 98308
  17.9 13.2 %copy-start.12 = (bf16[64,256]{1,0:T(8,128)(2,1)S(1)}, bf16[64,256]{1,0:T(8,128)(2,1)}, u32[]{:S(2)}) copy-start(bf16[64,256]{1,0:T(8,128)(2,1)} %constant.17.clone.ll) | copy-start | bytes 98308
  18.0 1.0 copy-start.18
  18.9 0.8 copy-start.19
  23.0 1.9 %copy-start.22 = (s32[32,128]{1,0:T(8,128)}, s32[32,128]{1,0:T(8,128)S(1)}, u32[]{:S(2)}) copy-start(s32[32,128]{1,0:T(8,128)S(1)} %get-tuple-element.35.slot_lane) | copy-start | bytes 49156
  25.0 34.5 %all-to-all-start.1 = ((s16[4,576,256]{2,1,0:T(8,128)(2,1)}), s16[4,576,256]{2,1,0:T(8,128)(2,1)S(1)}, u32[]{:S(2)}, u32[]{:S(2)}) async-start(s16[4,576,256]{2,1,0:T(8,128)(2,1)} %broadcast_in_dim.2), calls=%async_computation.1 | async-start | bytes 2359296 | tf_op jit(solution)/shard_map/all_to_all | solution.py:338
  31.1 1.2 %copy-start.1 = (f32[256,1024]{1,0:T(8,128)S(1)}, f32[256,1024]{1,0:T(8,128)}, u32[]{:S(2)}) copy-start(f32[256,1024]{1,0:T(8,128)} %momentum.3) | copy-start | bytes 3145732
  33.7 0.8 copy-start.3
  59.5 9.3 %copy-start.26 = (s32[8,128]{1,0:T(8,128)S(1)}, s32[8,128]{1,0:T(8,128)}, u32[]{:S(2)}) copy-start(s32[8,128]{1,0:T(8,128)} %copy-done.25) | copy-start | bytes 12292
  59.5 9.3 %collective-permute-start = (s16[2304,256]{1,0:T(8,128)(2,1)S(1)}, s16[2304,256]{1,0:T(8,128)(2,1)S(1)}, u32[]{:S(2)}, u32[]{:S(2)}) collective-permute-start(s16[2304,256]{1,0:T(8,128)(2,1)S(1)} %bitcast.10), channel_id=1, source_target_pairs={{0,1},{1,0},{2,3},{3,2},{4,5},{5,4},{6,7},{7,6},{8,9},{9,8},{10,11... | collective-permute-start | bytes 3538952 | tf_op jit(solution)/shard_map/ppermute | solution.py:364
  65.2 1.1 copy-start.4
  66.2 1.0 copy-start.6
  67.3 0.8 copy-start.17
  70.7 38.1 %all-to-all-start.2 = ((f32[512,1,128]{2,1,0:T(1,128)}), f32[512,1,128]{2,1,0:T(1,128)S(1)}, u32[]{:S(2)}, u32[]{:S(2)}) async-start(f32[512,1,128]{2,1,0:T(1,128)} %bitcast.7), calls=%async_computation.2 | async-start | bytes 524288 | tf_op jit(solution)/shard_map/all_to_all | solution.py:370
  86.7 1.2 %copy-start.2 = (f32[256,1024]{1,0:T(8,128)S(1)}, f32[256,1024]{1,0:T(8,128)}, u32[]{:S(2)}) copy-start(f32[256,1024]{1,0:T(8,128)} %momentum.3) | copy-start | bytes 3145732
  87.9 0.8 copy-start.15
  89.7 1.4 %copy-start.7 = (bf16[8,256,512]{2,1,0:T(8,128)(2,1)}, bf16[8,256,512]{2,1,0:T(8,128)(2,1)S(1)}, u32[]{:S(2)}) copy-start(bf16[8,256,512]{2,1,0:T(8,128)(2,1)S(1)} %get-tuple-element.38.turned) | copy-start | bytes 6291460
  91.0 1.0 copy-start.8
  102.9 5.9 %copy-start.13 = (f32[512,128]{1,0:T(8,128)S(1)}, f32[512,128]{1,0:T(8,128)}, u32[]{:S(2)}) copy-start(f32[512,128]{1,0:T(8,128)} %constant.18.clone.weights) | copy-start | bytes 786436
  (9 other events, 6.1 us)
Sparse Core Ops, SparseCore 0:
  10.1 92.7 all-gather.1

commit v5 on v4

--- a/solution.py
+++ b/solution.py
@@ -12,7 +12,7 @@
 ROWS = 256
 WIDTH = 1024
 TOKENS = 4096
-STEPS = 8
+STEPS = 4
 LEVELS = 32000.0
 SENT = 144
 F32 = jnp.float32
@@ -220,33 +220,27 @@
         base[:, cols] = 0.999 * momentum[:, cols] - dot3(split(back[:, q * 64:(q + 1) * 64]), left)
 
 
-def final_kernel(turned, grads, base, out, done, sides, held, start, sems):
+def final_kernel(turned, grads, base, *refs):
+    sources, (out, update), (sides, held, start), refs = refs[:5], refs[5:7], refs[7:10], refs[10:]
+    (received, index, weights, lh, ll), (first, second, wide, rows, sems) = refs[:5], refs[5:]
     size = TOKENS // STEPS
-    first = pltpu.make_async_copy(base, start, sems.at[2 * STEPS])
+    last = 2 * STEPS
+    small = [pltpu.make_async_copy(x, y, sems.at[last + 1 + k]) for k, (x, y) in enumerate(zip(sources, refs[:5]))]
+    small.append(pltpu.make_async_copy(base, start, sems.at[last]))
+    for copy in small:
+        copy.start()
     copies = []
     for k in range(STEPS):
-        rows = pl.ds(k * size, size)
+        part = pl.ds(k * size, size)
         copies.append((
             pltpu.make_async_copy(turned.at[k], sides.at[k], sems.at[STEPS + k]),
-            pltpu.make_async_copy(grads.at[rows], held.at[rows], sems.at[k]),
+            pltpu.make_async_copy(grads.at[part], held.at[part], sems.at[k]),
         ))
         for copy in copies[k]:
             copy.start()
-        if k == 0:
-            first.start()
-    done[...] = jnp.zeros((8, 128), F32)
-    for k in range(STEPS):
-        for copy in copies[k]:
-            copy.wait()
-        if k == 0:
-            first.wait()
-        rows = slice(k * size, (k + 1) * size)
-        for q in range(4):
-            cols = slice(q * 256, (q + 1) * 256)
-            out[:, cols] = (start if k == 0 else out)[:, cols] + dot(sides[k], held[rows, cols])
-
-
-def decode_kernel(received, index, weights, lh, ll, done, out, first, second, wide):
+
+    for copy in small:
+        copy.wait()
     total = received[0:32, :]
     for r in range(1, 16):
         total = total + received[r * 32:(r + 1) * 32, :]
@@ -264,14 +258,25 @@
             piece = columns[:, f * 64:(f + 1) * 64]
             wide[q * 4 + f] = jnp.concatenate([piece, piece], axis=1)
 
-    @pl.loop(0, CH // 2)
+    @pl.loop(0, CH // 2, unroll=4)
     def _(pair):
         row = pl.multiple_of(pair * BAND, BAND)
         factors = weights[pl.ds(row, BAND), :]
         value = wide[0] * factors[0:1]
         for f in range(1, BAND):
             value = value + wide[f] * factors[f:f + 1]
-        out[:, pl.ds(pl.multiple_of(pair * 128, 128), 128)] = value.astype(BF16)
+        rows[:, pl.ds(pl.multiple_of(pair * 128, 128), 128)] = value.astype(BF16)
+
+    decoded = pltpu.make_async_copy(rows, update, sems.at[last + 6])
+    decoded.start()
+    for k in range(STEPS):
+        for copy in copies[k]:
+            copy.wait()
+        part = slice(k * size, (k + 1) * size)
+        for q in range(4):
+            cols = slice(q * 256, (q + 1) * 256)
+            out[:, cols] = (start if k == 0 else out)[:, cols] + dot(sides[k], held[part, cols])
+    decoded.wait()
 
 
 def vmem(n):
@@ -295,34 +300,26 @@
     )(*args)
 
 
-def final(turned, grads, base):
+def final(turned, grads, base, received, index, lh, ll):
+    table = band_table().T.reshape(CH // 2, 2, BAND).transpose(0, 2, 1)
+    weights = np.repeat(table, 64, axis=2).reshape(CH // 2 * BAND, 128).astype(np.float32)
     return pl.pallas_call(
         final_kernel,
-        out_shape=(sds((ROWS, WIDTH)), sds((8, 128))),
-        in_specs=[pl.BlockSpec(memory_space=pl.ANY)] * 3,
-        out_specs=tuple(vmem(2)),
+        out_shape=(sds((ROWS, WIDTH)), sds((64, CH * CH), BF16)),
+        in_specs=[pl.BlockSpec(memory_space=pl.ANY)] * 8,
+        out_specs=(vmem(1)[0], pl.BlockSpec(memory_space=pl.ANY)),
         scratch_shapes=[
             pltpu.VMEM((STEPS, ROWS, TOKENS // STEPS), BF16), pltpu.VMEM((TOKENS, WIDTH), BF16),
-            pltpu.VMEM((ROWS, WIDTH), F32), pltpu.SemaphoreType.DMA((2 * STEPS + 1,)),
+            pltpu.VMEM((ROWS, WIDTH), F32),
+            pltpu.VMEM((512, 128), F32), pltpu.VMEM((64, 256), I32), pltpu.VMEM((CH // 2 * BAND, 128), F32),
+            pltpu.VMEM((64, 256), BF16), pltpu.VMEM((64, 256), BF16),
+            pltpu.VMEM((64, 128), F32), pltpu.VMEM((64, 128), F32), pltpu.VMEM((BAND, 64, 128), F32),
+            pltpu.VMEM((64, CH * CH), BF16), pltpu.SemaphoreType.DMA((2 * STEPS + 7,)),
         ],
         compiler_params=pltpu.CompilerParams(vmem_limit_bytes=56 << 20),
         cost_estimate=pl.CostEstimate(flops=2 * TOKENS * ROWS * WIDTH, bytes_accessed=14 << 20, transcendentals=0),
         name="final",
-    )(turned, grads, base)
-
-
-def decode(received, index, lh, ll, done):
-    table = band_table().T.reshape(CH // 2, 2, BAND).transpose(0, 2, 1)
-    weights = np.repeat(table, 64, axis=2).reshape(CH // 2 * BAND, 128).astype(np.float32)
-    return pl.pallas_call(
-        decode_kernel,
-        out_shape=sds((64, CH * CH), BF16),
-        in_specs=vmem(5) + [pl.BlockSpec(memory_space=pl.ANY)],
-        out_specs=vmem(1)[0],
-        scratch_shapes=[pltpu.VMEM((64, 128), F32)] * 2 + [pltpu.VMEM((BAND, 64, 128), F32)],
-        compiler_params=pltpu.CompilerParams(vmem_limit_bytes=24 << 20),
-        name="decode",
-    )(received, index, weights, lh, ll, done)
+    )(turned, grads, base, received, index, weights, lh, ll)
 
 
 def shard(z, x, c):
@@ -372,9 +369,7 @@
         ready_kernel, (sds((STEPS, ROWS, TOKENS // STEPS), BF16), sds((ROWS, WIDTH))),
         activations, momentum, coef, mask, lh, ll, th, tl,
     )
-    new_momentum, done = final(turned, all_grads, base)
-    received, done = lax.optimization_barrier((received, done))
-    update = decode(received, index, lh, ll, done)
+    new_momentum, update = final(turned, all_grads, base, received, index, lh, ll)
     return (new_momentum, update)
 
 

time: 120 us -> 119 us (level)
  Pallas kernels: 16.4 us -> 14.6 us
  waiting for transfers between devices: 36 us -> 37.5 us
    all_to_all x1, waiting for transfers between devices: 0.01 us -> 12.4 us  [body(): received = lax.all_to_all(board, ('rep', 'shard'), 0, 0, tiled=True)]
    all_gather x1, waiting for transfers between devices: 10.9 us -> 0.01 us  [body(): all_grads = lax.all_gather(key_grads, 'shard', axis=0, tiled=True)]
    pallas_call x2 -> x1, Pallas kernels: 8.69 us -> 6.87 us  [final(): pl.pallas_call(final_kernel, out_shape=(sds((ROWS, WIDTH)), sds((64, CH *...]
    unnamed x56 -> x52, local copies, waits for them, and re-layouts: 15.8 us -> 15 us
  transfers between devices with their start and end apart: 5 -> 5, of which waited for: 3 -> 3; matrix products, arithmetic and copies ran while one was open for 1% -> 1% of each run, Pallas kernels for 11% -> 7%
where the time goes in v5:
time: 119 us; the launch traced here: 118 us
  waiting for transfers between devices  37.5 us (32%)
  starting transfers between devices  35.6 us (30%)
  local copies, waits for them, and re-layouts  16.1 us (14%)
  Pallas kernels  14.6 us (12%)
  between operations  14.2 us (12%)
    all_to_all x2, waiting for transfers between devices, exchange(): lax.all_to_all(copies, 'shard', 0, 0, tiled=True, axis_index_groups=groups)  24.4 us
    all_to_all x1, starting transfers between devices, body(): received = lax.all_to_all(board, ('rep', 'shard'), 0, 0, tiled=True)  16 us
    unnamed x52, local copies, waits for them, and re-layouts  15 us
    all_to_all x2, starting transfers between devices, exchange(): lax.all_to_all(copies, 'shard', 0, 0, tiled=True, axis_index_groups=groups)  13.9 us
    all_to_all x1, waiting for transfers between devices, body(): received = lax.all_to_all(board, ('rep', 'shard'), 0, 0, tiled=True)  12.4 us
    pallas_call x6, Pallas kernels, call(): pl.pallas_call(kernel, out_shape=shapes, in_specs=scalar + vmem(len(args)...  7.68 us
    pallas_call x1, Pallas kernels, final(): pl.pallas_call(final_kernel, out_shape=(sds((ROWS, WIDTH)), sds((64, CH *...  6.87 us
    ppermute x1, starting transfers between devices, body(): other = lax.ppermute(own, 'shard', OTHER_CORE)  5.69 us
  transfers between devices with their start and end apart: 5, of which 3 were waited for; matrix products, arithmetic and copies ran while one was open for 1% of the time, Pallas kernels for 7%

profile of v5, /device:TPU:1, one launch (start us, length us, event | category | flops | bytes accessed | tf_op | source)
XLA Modules:
  0.0 118.0 jit_solution(9233989038439263569)
XLA Ops:
  7.9 2.2 %project_kernel.1 = s16[576,256]{1,0:T(8,128)(2,1)} custom-call(bf16[128,1024]{1,0:T(8,128)(2,1)} %grads.1, bf16[256,64]{1,0:T(8,128)(2,1)} %constant.14.clone.th, bf16[256,64]{1,0:T(8,128)(2,1)} %constant.15.clone.tl), custom_call_target="tpu_custom_call" | custom-call | tf_op jit(solution)/shard_map/project_kernel/pallas_call | solution.py:293
  10.1 7.8 %all-to-all-start = ((s16[4,144,256]{2,1,0:T(8,128)(2,1)}), s16[4,144,256]{2,1,0:T(8,128)(2,1)S(1)}, u32[]{:S(2)}, u32[]{:S(2)}) async-start(s16[4,144,256]{2,1,0:T(8,128)(2,1)} %bitcast.15), calls=%async_computation | async-start | bytes 589824 | tf_op jit(solution)/shard_map/all_to_all | solution.py:335
  18.0 1.0 copy-done.16
  19.0 0.8 copy-done.17
  23.0 0.8 all-to-all-done
  23.8 1.1 broadcast_in_dim.2
  25.0 6.1 %all-to-all-start.1 = ((s16[4,576,256]{2,1,0:T(8,128)(2,1)}), s16[4,576,256]{2,1,0:T(8,128)(2,1)S(1)}, u32[]{:S(2)}, u32[]{:S(2)}) async-start(s16[4,576,256]{2,1,0:T(8,128)(2,1)} %broadcast_in_dim.2), calls=%async_computation.1 | async-start | bytes 2359296 | tf_op jit(solution)/shard_map/all_to_all | solution.py:335
  31.1 1.2 %copy-done.1 = f32[256,1024]{1,0:T(8,128)S(1)} copy-done((f32[256,1024]{1,0:T(8,128)S(1)}, f32[256,1024]{1,0:T(8,128)}, u32[]{:S(2)}) %copy-start.1) | copy-done | bytes 1048600
  32.3 1.4 %prepare_kernel.1 = (bf16[2,64,2048]{2,1,0:T(8,128)(2,1)S(1)}, bf16[2,64,2048]{2,1,0:T(8,128)(2,1)S(1)}, f32[64,256]{1,0:T(8,128)S(1)}) custom-call(bf16[4096,256]{1,0:T(8,128)(2,1)S(1)} %copy-done, f32[256,1024]{1,0:T(8,128)S(1)} %copy-done.1, bf16[64,256]{1,0:T(8,128)(2,1)S(1)} %copy-done.11, bf16[64,256]{1,0:T(8,128)(2,1)S(1)} %copy-done.12, ...), custom_call_target="tpu_custom_call" | custom-call | tf_op jit(solution)/shard_map/prepare_kernel/pallas_call | solution.py:293
  33.7 0.8 copy-done.3
  34.5 0.8 copy-done.5
  35.9 23.6 %all-to-all-done.1 = s16[4,576,256]{2,1,0:T(8,128)(2,1)S(1)} async-done(((s16[4,576,256]{2,1,0:T(8,128)(2,1)}), s16[4,576,256]{2,1,0:T(8,128)(2,1)S(1)}, u32[]{:S(2)}, u32[]{:S(2)}) %all-to-all-start.1) | async-done | bytes 1179680 | tf_op jit(solution)/shard_map/all_to_all | solution.py:335
  59.5 5.7 %collective-permute-start = (s16[2304,256]{1,0:T(8,128)(2,1)S(1)}, s16[2304,256]{1,0:T(8,128)(2,1)S(1)}, u32[]{:S(2)}, u32[]{:S(2)}) collective-permute-start(s16[2304,256]{1,0:T(8,128)(2,1)S(1)} %bitcast.10), channel_id=1, source_target_pairs={{0,1},{1,0},{2,3},{3,2},{4,5},{5,4},{6,7},{7,6},{8,9},{9,8},{10,11... | collective-permute-start | bytes 3538952 | tf_op jit(solution)/shard_map/ppermute | solution.py:361
  65.2 1.0 copy-done.4
  66.2 1.0 copy-done.6
  67.3 0.8 copy-done.15
  68.9 1.9 %far_kernel.1 = (f32[64,256]{1,0:T(8,128)S(1)}, f32[512,128]{1,0:T(8,128)}) custom-call(s32[1]{0:T(128)} %bitcast.place, bf16[2,64,2048]{2,1,0:T(8,128)(2,1)S(1)} %copy-done.4, bf16[2,64,2048]{2,1,0:T(8,128)(2,1)S(1)} %copy-done.6, s16[2304,256]{1,0:T(8,128)(2,1)S(1)} %collective-permute-done.other, f32[64,256]{1,0:T(8,128)S(1)} %near_kernel.1.near, ...), custom_call_target="tpu_custom_call" | custom-call | tf_op jit(solution)/shard_map/far_kernel/pallas_call | solution.py:293
  70.7 16.0 %all-to-all-start.2 = ((f32[512,1,128]{2,1,0:T(1,128)}), f32[512,1,128]{2,1,0:T(1,128)S(1)}, u32[]{:S(2)}, u32[]{:S(2)}) async-start(f32[512,1,128]{2,1,0:T(1,128)} %bitcast.7), calls=%async_computation.2 | async-start | bytes 524288 | tf_op jit(solution)/shard_map/all_to_all | solution.py:367
  86.7 1.2 %copy-done.2 = f32[256,1024]{1,0:T(8,128)S(1)} copy-done((f32[256,1024]{1,0:T(8,128)S(1)}, f32[256,1024]{1,0:T(8,128)}, u32[]{:S(2)}) %copy-start.2) | copy-done | bytes 1048600
  87.9 0.9 ready_kernel.1
  88.8 1.4 %copy-done.7 = bf16[4,256,1024]{2,1,0:T(8,128)(2,1)} copy-done((bf16[4,256,1024]{2,1,0:T(8,128)(2,1)}, bf16[4,256,1024]{2,1,0:T(8,128)(2,1)S(1)}, u32[]{:S(2)}) %copy-start.7) | copy-done | bytes 2097176
  90.2 1.0 copy-done.8
  91.2 12.4 %all-to-all-done.2 = f32[512,1,128]{2,1,0:T(1,128)S(1)} async-done(((f32[512,1,128]{2,1,0:T(1,128)}), f32[512,1,128]{2,1,0:T(1,128)S(1)}, u32[]{:S(2)}, u32[]{:S(2)}) %all-to-all-start.2) | async-done | bytes 262176 | tf_op jit(solution)/shard_map/all_to_all | solution.py:367
  104.2 6.9 %final.1 = (f32[256,1024]{1,0:T(8,128)}, bf16[64,4096]{1,0:T(8,128)(2,1)}) custom-call(bf16[4,256,1024]{2,1,0:T(8,128)(2,1)} %copy-done.7, bf16[4096,1024]{1,0:T(8,128)(2,1)} %all-gather.2.cloned.1.call-done.grads, f32[256,1024]{1,0:T(8,128)} %copy-done.8, f32[512,128]{1,0:T(8,128)} %bitcast.16, s32[64,256]{1,0:T(8,128)} %copy-done.13, ...), custom_call_target="tpu_custom_call" | custom-call | flops 2147483648 | bytes 14680064 | tf_op jit(solution)/shard_map/final/pallas_call | solution.py:306
  (47 shorter events, 6.0 us)
Async XLA Ops:
  7.2 96.4 %all-gather.2.cloned.1.call-start = ((), (), s32[]{:S(2)}) async-start(), calls=%async_computation.3 | async-start | bytes 8650752 | tf_op jit(solution)/shard_map/all_gather | solution.py:342
  10.1 13.7 %all-to-all-start = ((s16[4,144,256]{2,1,0:T(8,128)(2,1)}), s16[4,144,256]{2,1,0:T(8,128)(2,1)S(1)}, u32[]{:S(2)}, u32[]{:S(2)}) async-start(s16[4,144,256]{2,1,0:T(8,128)(2,1)} %bitcast.15), calls=%async_computation | async-start | bytes 589824 | tf_op jit(solution)/shard_map/all_to_all | solution.py:335
  17.9 13.2 %copy-start = (bf16[4096,256]{1,0:T(8,128)(2,1)S(1)}, bf16[4096,256]{1,0:T(8,128)(2,1)}, u32[]{:S(2)}) copy-start(bf16[4096,256]{1,0:T(8,128)(2,1)} %inputs.3) | copy-start | bytes 6291460
  17.9 13.2 %copy-start.9 = (bf16[256,64]{1,0:T(8,128)(2,1)S(1)}, bf16[256,64]{1,0:T(8,128)(2,1)}, u32[]{:S(2)}) copy-start(bf16[256,64]{1,0:T(8,128)(2,1)} %constant.15.clone.tl) | copy-start | bytes 98308
  17.9 13.2 %copy-start.10 = (bf16[256,64]{1,0:T(8,128)(2,1)S(1)}, bf16[256,64]{1,0:T(8,128)(2,1)}, u32[]{:S(2)}) copy-start(bf16[256,64]{1,0:T(8,128)(2,1)} %constant.14.clone.th) | copy-start | bytes 98308
  17.9 13.2 %copy-start.11 = (bf16[64,256]{1,0:T(8,128)(2,1)S(1)}, bf16[64,256]{1,0:T(8,128)(2,1)}, u32[]{:S(2)}) copy-start(bf16[64,256]{1,0:T(8,128)(2,1)} %constant.16.clone.lh.refs_3_) | copy-start | bytes 98308
  17.9 13.2 %copy-start.12 = (bf16[64,256]{1,0:T(8,128)(2,1)S(1)}, bf16[64,256]{1,0:T(8,128)(2,1)}, u32[]{:S(2)}) copy-start(bf16[64,256]{1,0:T(8,128)(2,1)} %constant.17.clone.ll.refs_4_) | copy-start | bytes 98308
  18.0 1.0 copy-start.16
  18.9 0.8 copy-start.17
  23.0 2.0 %copy-start.13 = (s32[64,256]{1,0:T(8,128)}, s32[64,256]{1,0:T(8,128)S(1)}, u32[]{:S(2)}) copy-start(s32[64,256]{1,0:T(8,128)S(1)} %get-tuple-element.37.refs_1_) | copy-start | bytes 196612
  25.0 34.5 %all-to-all-start.1 = ((s16[4,576,256]{2,1,0:T(8,128)(2,1)}), s16[4,576,256]{2,1,0:T(8,128)(2,1)S(1)}, u32[]{:S(2)}, u32[]{:S(2)}) async-start(s16[4,576,256]{2,1,0:T(8,128)(2,1)} %broadcast_in_dim.2), calls=%async_computation.1 | async-start | bytes 2359296 | tf_op jit(solution)/shard_map/all_to_all | solution.py:335
  31.1 1.2 %copy-start.1 = (f32[256,1024]{1,0:T(8,128)S(1)}, f32[256,1024]{1,0:T(8,128)}, u32[]{:S(2)}) copy-start(f32[256,1024]{1,0:T(8,128)} %momentum.3) | copy-start | bytes 3145732
  33.7 0.8 copy-start.3
  34.5 0.8 copy-start.5
  59.5 9.3 %copy-start.24 = (s32[8,128]{1,0:T(8,128)S(1)}, s32[8,128]{1,0:T(8,128)}, u32[]{:S(2)}) copy-start(s32[8,128]{1,0:T(8,128)} %copy-done.23) | copy-start | bytes 12292
  59.5 9.3 %collective-permute-start = (s16[2304,256]{1,0:T(8,128)(2,1)S(1)}, s16[2304,256]{1,0:T(8,128)(2,1)S(1)}, u32[]{:S(2)}, u32[]{:S(2)}) collective-permute-start(s16[2304,256]{1,0:T(8,128)(2,1)S(1)} %bitcast.10), channel_id=1, source_target_pairs={{0,1},{1,0},{2,3},{3,2},{4,5},{5,4},{6,7},{7,6},{8,9},{9,8},{10,11... | collective-permute-start | bytes 3538952 | tf_op jit(solution)/shard_map/ppermute | solution.py:361
  65.2 1.1 copy-start.4
  66.2 1.0 copy-start.6
  67.3 0.8 copy-start.15
  68.1 0.7 copy-start.21
  70.7 32.8 %all-to-all-start.2 = ((f32[512,1,128]{2,1,0:T(1,128)}), f32[512,1,128]{2,1,0:T(1,128)S(1)}, u32[]{:S(2)}, u32[]{:S(2)}) async-start(f32[512,1,128]{2,1,0:T(1,128)} %bitcast.7), calls=%async_computation.2 | async-start | bytes 524288 | tf_op jit(solution)/shard_map/all_to_all | solution.py:367
  86.7 1.2 %copy-start.2 = (f32[256,1024]{1,0:T(8,128)S(1)}, f32[256,1024]{1,0:T(8,128)}, u32[]{:S(2)}) copy-start(f32[256,1024]{1,0:T(8,128)} %momentum.3) | copy-start | bytes 3145732
  88.8 1.4 %copy-start.7 = (bf16[4,256,1024]{2,1,0:T(8,128)(2,1)}, bf16[4,256,1024]{2,1,0:T(8,128)(2,1)S(1)}, u32[]{:S(2)}) copy-start(bf16[4,256,1024]{2,1,0:T(8,128)(2,1)S(1)} %get-tuple-element.34.turned) | copy-start | bytes 6291460
  90.2 1.0 copy-start.8
  (7 other events, 4.5 us)
Sparse Core Ops, SparseCore 0:
  10.1 92.7 all-gather.1

commit v6 on v5

--- a/solution.py
+++ b/solution.py
@@ -15,6 +15,7 @@
 STEPS = 4
 LEVELS = 32000.0
 SENT = 144
+PACKED = 528
 F32 = jnp.float32
 BF16 = jnp.bfloat16
 I32 = jnp.int32
@@ -163,12 +164,25 @@
         kept[:, q * 64:(q + 1) * 64] = dot3(split(half[:, q * 256:(q + 1) * 256]), right)
 
 
+def repack_kernel(along_z, out):
+    row = iota((16, 256), 0)
+    scales = jnp.zeros((16, 256), I32)
+    for z in range(4):
+        scales = jnp.where(row == z, along_z[z * SENT + 128:(z + 1) * SENT, :].astype(I32), scales)
+    scales = scales.astype(jnp.int16)
+    for x in range(4):
+        for z in range(4):
+            out[x * PACKED + z * 128:x * PACKED + (z + 1) * 128, :] = along_z[z * SENT:z * SENT + 128, :]
+        out[x * PACKED + 512:(x + 1) * PACKED, :] = scales
+
+
 def contract(high, low, side, source):
     total = jnp.zeros((64, 256), F32)
     for k in range(16):
-        at, to = k * SENT, k * 128
+        x, z = k // 4, k % 4
+        at, to = x * PACKED + z * 128, k * 128
         xh, xl = split(source[at:at + 128, :].astype(I32).astype(F32))
-        scale = power(source[at + 128:at + 144, :].astype(I32).astype(F32)[:1, :128]).astype(BF16)
+        scale = power(source[x * PACKED + 512:(x + 1) * PACKED, :].astype(I32).astype(F32)[z:z + 1, :128]).astype(BF16)
         left = jnp.concatenate([high[side, :, to:to + 128], low[side, :, to:to + 128]], axis=0)
         left = left * jnp.broadcast_to(scale, (128, 128))
         both = dot(left, xh)
@@ -201,12 +215,15 @@
     return board
 
 
-def far_kernel(place, high, low, other, near, col_index, row_pick, slot_row, slot_lane, coef, sent):
+def far_kernel(place, high, low, other, near, col_index, row_pick, slot_row, slot_lane, coef, sent, held, sem):
     total = near[...] + contract(high, low, 1 - (place[0] & 1), other)
-    coef[...] = total
+    held[...] = total
+    copy = pltpu.make_async_copy(held, coef, sem.at[0])
+    copy.start()
     board = select(total[:, :128], total[:, 128:], col_index, row_pick, slot_row, slot_lane)
     for r in range(16):
         sent[r * 32:(r + 1) * 32, :] = board
+    copy.wait()
 
 
 def ready_kernel(inputs, momentum, coef, mask, lh, ll, th, tl, turned, base):
@@ -297,6 +314,18 @@
         out_specs=tuple(vmem(len(shapes))) if many else vmem(1)[0],
         compiler_params=pltpu.CompilerParams(vmem_limit_bytes=limit << 20),
         name=kernel.__name__,
+    )(*args)
+
+
+def far(*args):
+    return pl.pallas_call(
+        far_kernel,
+        out_shape=(sds((64, 256)), sds((512, 128))),
+        in_specs=[pl.BlockSpec(memory_space=pltpu.SMEM)] + vmem(len(args) - 1),
+        out_specs=(pl.BlockSpec(memory_space=pl.ANY), vmem(1)[0]),
+        scratch_shapes=[pltpu.VMEM((64, 256), F32), pltpu.SemaphoreType.DMA((1,))],
+        compiler_params=pltpu.CompilerParams(vmem_limit_bytes=40 << 20),
+        name="far",
     )(*args)
 
 
@@ -350,7 +379,7 @@
         place, jnp.transpose(freq_rows, (1, 2, 0)), jnp.transpose(freq_cols, (1, 2, 0)), dispatch, scalars=1,
     )
     along_z, slot_row, after = lax.optimization_barrier((along_z, slot_row, jnp.asarray(lh)))
-    own = exchange(jnp.broadcast_to(along_z[None], (4, 4 * SENT, 256)).reshape(16 * SENT, 256), ALONG_X)
+    own = exchange(call(repack_kernel, sds((4 * PACKED, 256), jnp.int16), along_z), ALONG_X)
     high, low, kept = call(
         prepare_kernel,
         (sds((2, 64, 2048), BF16), sds((2, 64, 2048), BF16), sds((64, 256))),
@@ -360,10 +389,7 @@
 
     other = lax.ppermute(own, "shard", OTHER_CORE)
     near = call(near_kernel, sds((64, 256)), place, high, low, own, kept, scalars=1)
-    coef, board = call(
-        far_kernel, (sds((64, 256)), sds((512, 128))),
-        place, high, low, other, near, col_index, row_pick, slot_row, slot_lane, scalars=1,
-    )
+    coef, board = far(place, high, low, other, near, col_index, row_pick, slot_row, slot_lane)
     received = lax.all_to_all(board, ("rep", "shard"), 0, 0, tiled=True)
     turned, base = call(
         ready_kernel, (sds((STEPS, ROWS, TOKENS // STEPS), BF16), sds((ROWS, WIDTH))),

time: 119 us -> 117 us (0.983)
  local copies, waits for them, and re-layouts: 16.1 us -> 13.6 us
    pallas_call x0 -> x1, Pallas kernels: none -> 1.98 us  [far(): pl.pallas_call(far_kernel, out_shape=(sds((64, 256)), sds((512, 128))), i...]
    pallas_call x6, Pallas kernels: 7.68 us -> 5.88 us  [call(): pl.pallas_call(kernel, out_shape=shapes, in_specs=scalar + vmem(len(args)...]
    unnamed x52 -> x46, local copies, waits for them, and re-layouts: 15 us -> 13.6 us
  transfers between devices with their start and end apart: 5 -> 5, of which waited for: 3 -> 4; matrix products, arithmetic and copies ran while one was open for 1% -> 0% of each run, Pallas kernels for 7% -> 7%
where the time goes in v6:
time: 117 us; the launch traced here: 116 us
  waiting for transfers between devices  37.7 us (32%)
  starting transfers between devices  35.7 us (31%)
  Pallas kernels  14.7 us (13%)
  between operations  14.2 us (12%)
  local copies, waits for them, and re-layouts  13.6 us (12%)
    all_to_all x2, waiting for transfers between devices, exchange(): lax.all_to_all(copies, 'shard', 0, 0, tiled=True, axis_index_groups=groups)  23.8 us
    all_to_all x1, starting transfers between devices, body(): received = lax.all_to_all(board, ('rep', 'shard'), 0, 0, tiled=True)  16 us
    all_to_all x2, starting transfers between devices, exchange(): lax.all_to_all(copies, 'shard', 0, 0, tiled=True, axis_index_groups=groups)  14.1 us
    unnamed x46, local copies, waits for them, and re-layouts  13.6 us
    all_to_all x1, waiting for transfers between devices, body(): received = lax.all_to_all(board, ('rep', 'shard'), 0, 0, tiled=True)  12.4 us
    pallas_call x1, Pallas kernels, final(): pl.pallas_call(final_kernel, out_shape=(sds((ROWS, WIDTH)), sds((64, CH *...  6.88 us
    pallas_call x6, Pallas kernels, call(): pl.pallas_call(kernel, out_shape=shapes, in_specs=scalar + vmem(len(args)...  5.88 us
    ppermute x1, starting transfers between devices, body(): other = lax.ppermute(own, 'shard', OTHER_CORE)  5.56 us
  transfers between devices with their start and end apart: 5, of which 4 were waited for; matrix products, arithmetic and copies ran while one was open for 0% of the time, Pallas kernels for 7%

profile of v6, /device:TPU:1, one launch (start us, length us, event | category | flops | bytes accessed | tf_op | source)
XLA Modules:
  0.0 116.0 jit_solution(13696040731033364682)
XLA Ops:
  7.9 2.2 %project_kernel.1 = s16[576,256]{1,0:T(8,128)(2,1)} custom-call(bf16[128,1024]{1,0:T(8,128)(2,1)} %grads.1, bf16[256,64]{1,0:T(8,128)(2,1)} %constant.14.clone.th, bf16[256,64]{1,0:T(8,128)(2,1)} %constant.15.clone.tl), custom_call_target="tpu_custom_call" | custom-call | tf_op jit(solution)/shard_map/project_kernel/pallas_call | solution.py:310
  10.1 8.0 %all-to-all-start = ((s16[4,144,256]{2,1,0:T(8,128)(2,1)}), s16[4,144,256]{2,1,0:T(8,128)(2,1)S(1)}, u32[]{:S(2)}, u32[]{:S(2)}) async-start(s16[4,144,256]{2,1,0:T(8,128)(2,1)} %bitcast.17), calls=%async_computation | async-start | bytes 589824 | tf_op jit(solution)/shard_map/all_to_all | solution.py:364
  18.1 0.8 copy-done.17
  18.9 0.8 copy-done.18
  22.4 1.6 %all-to-all-done = s16[4,144,256]{2,1,0:T(8,128)(2,1)S(1)} async-done(((s16[4,144,256]{2,1,0:T(8,128)(2,1)}), s16[4,144,256]{2,1,0:T(8,128)(2,1)S(1)}, u32[]{:S(2)}, u32[]{:S(2)}) %all-to-all-start) | async-done | bytes 294944 | tf_op jit(solution)/shard_map/all_to_all | solution.py:364
  24.1 1.0 copy-done.1
  25.1 6.1 %all-to-all-start.1 = ((s16[4,528,256]{2,1,0:T(8,128)(2,1)}), s16[4,528,256]{2,1,0:T(8,128)(2,1)S(1)}, u32[]{:S(2)}, u32[]{:S(2)}) async-start(s16[4,528,256]{2,1,0:T(8,128)(2,1)} %bitcast.13), calls=%async_computation.1 | async-start | bytes 2162688 | tf_op jit(solution)/shard_map/all_to_all | solution.py:364
  31.3 1.2 %copy-done.2 = f32[256,1024]{1,0:T(8,128)S(1)} copy-done((f32[256,1024]{1,0:T(8,128)S(1)}, f32[256,1024]{1,0:T(8,128)}, u32[]{:S(2)}) %copy-start.2) | copy-done | bytes 1048600
  32.5 1.4 %prepare_kernel.1 = (bf16[2,64,2048]{2,1,0:T(8,128)(2,1)S(1)}, bf16[2,64,2048]{2,1,0:T(8,128)(2,1)S(1)}, f32[64,256]{1,0:T(8,128)S(1)}) custom-call(bf16[4096,256]{1,0:T(8,128)(2,1)S(1)} %copy-done, f32[256,1024]{1,0:T(8,128)S(1)} %copy-done.2, bf16[64,256]{1,0:T(8,128)(2,1)S(1)} %copy-done.14, bf16[64,256]{1,0:T(8,128)(2,1)S(1)} %copy-done.15, ...), custom_call_target="tpu_custom_call" | custom-call | tf_op jit(solution)/shard_map/prepare_kernel/pallas_call | solution.py:310
  33.8 0.8 copy-done.4
  34.6 0.8 copy-done.7
  35.4 22.2 %all-to-all-done.1 = s16[4,528,256]{2,1,0:T(8,128)(2,1)S(1)} async-done(((s16[4,528,256]{2,1,0:T(8,128)(2,1)}), s16[4,528,256]{2,1,0:T(8,128)(2,1)S(1)}, u32[]{:S(2)}, u32[]{:S(2)}) %all-to-all-start.1) | async-done | bytes 1081376 | tf_op jit(solution)/shard_map/all_to_all | solution.py:364
  57.6 5.6 %collective-permute-start = (s16[2112,256]{1,0:T(8,128)(2,1)S(1)}, s16[2112,256]{1,0:T(8,128)(2,1)S(1)}, u32[]{:S(2)}, u32[]{:S(2)}) collective-permute-start(s16[2112,256]{1,0:T(8,128)(2,1)S(1)} %bitcast.11), channel_id=1, source_target_pairs={{0,1},{1,0},{2,3},{3,2},{4,5},{5,4},{6,7},{7,6},{8,9},{9,8},{10,11... | collective-permute-start | bytes 3244040 | tf_op jit(solution)/shard_map/ppermute | solution.py:390
  63.2 1.0 copy-done.5
  64.2 1.1 copy-done.8
  66.5 2.0 %far.1 = (f32[64,256]{1,0:T(8,128)S(1)}, f32[512,128]{1,0:T(8,128)}) custom-call(s32[1]{0:T(128)} %bitcast.place, bf16[2,64,2048]{2,1,0:T(8,128)(2,1)S(1)} %copy-done.6, bf16[2,64,2048]{2,1,0:T(8,128)(2,1)S(1)} %copy-done.9, s16[2112,256]{1,0:T(8,128)(2,1)S(1)} %collective-permute-done.other, f32[64,256]{1,0:T(8,128)S(1)} %near_kernel.1.near, ...), custom_call_target="tpu_custom_call" | custom-call | tf_op jit(solution)/shard_map/far/pallas_call | solution.py:321
  68.5 16.0 %all-to-all-start.2 = ((f32[512,1,128]{2,1,0:T(1,128)}), f32[512,1,128]{2,1,0:T(1,128)S(1)}, u32[]{:S(2)}, u32[]{:S(2)}) async-start(f32[512,1,128]{2,1,0:T(1,128)} %bitcast.8), calls=%async_computation.2 | async-start | bytes 524288 | tf_op jit(solution)/shard_map/all_to_all | solution.py:393
  84.5 1.2 %copy-done.3 = f32[256,1024]{1,0:T(8,128)S(1)} copy-done((f32[256,1024]{1,0:T(8,128)S(1)}, f32[256,1024]{1,0:T(8,128)}, u32[]{:S(2)}) %copy-start.3) | copy-done | bytes 1048600
  85.7 0.9 ready_kernel.1
  86.6 1.4 %copy-done.10 = bf16[4,256,1024]{2,1,0:T(8,128)(2,1)} copy-done((bf16[4,256,1024]{2,1,0:T(8,128)(2,1)}, bf16[4,256,1024]{2,1,0:T(8,128)(2,1)S(1)}, u32[]{:S(2)}) %copy-start.10) | copy-done | bytes 2097176
  88.0 1.0 copy-done.11
  89.0 12.4 %all-to-all-done.2 = f32[512,1,128]{2,1,0:T(1,128)S(1)} async-done(((f32[512,1,128]{2,1,0:T(1,128)}), f32[512,1,128]{2,1,0:T(1,128)S(1)}, u32[]{:S(2)}, u32[]{:S(2)}) %all-to-all-start.2) | async-done | bytes 262176 | tf_op jit(solution)/shard_map/all_to_all | solution.py:393
  101.4 0.9 all-gather.2.cloned.1.call-done.grads
  102.2 6.9 %final.1 = (f32[256,1024]{1,0:T(8,128)}, bf16[64,4096]{1,0:T(8,128)(2,1)}) custom-call(bf16[4,256,1024]{2,1,0:T(8,128)(2,1)} %copy-done.10, bf16[4096,1024]{1,0:T(8,128)(2,1)} %all-gather.2.cloned.1.call-done.grads, f32[256,1024]{1,0:T(8,128)} %copy-done.11, f32[512,128]{1,0:T(8,128)} %bitcast.18, s32[64,256]{1,0:T(8,128)} %copy-done.16, ...), custom_call_target="tpu_custom_call" | custom-call | flops 2147483648 | bytes 14680064 | tf_op jit(solution)/shard_map/final/pallas_call | solution.py:335
  (41 shorter events, 4.7 us)
Async XLA Ops:
  7.2 95.1 %all-gather.2.cloned.1.call-start = ((), (), s32[]{:S(2)}) async-start(), calls=%async_computation.3 | async-start | bytes 8650752 | tf_op jit(solution)/shard_map/all_gather | solution.py:371
  10.1 21.1 %copy-start = (bf16[4096,256]{1,0:T(8,128)(2,1)S(1)}, bf16[4096,256]{1,0:T(8,128)(2,1)}, u32[]{:S(2)}) copy-start(bf16[4096,256]{1,0:T(8,128)(2,1)} %inputs.3) | copy-start | bytes 6291460
  10.1 21.1 %copy-start.12 = (bf16[256,64]{1,0:T(8,128)(2,1)S(1)}, bf16[256,64]{1,0:T(8,128)(2,1)}, u32[]{:S(2)}) copy-start(bf16[256,64]{1,0:T(8,128)(2,1)} %constant.15.clone.tl) | copy-start | bytes 98308
  10.1 21.1 %copy-start.13 = (bf16[256,64]{1,0:T(8,128)(2,1)S(1)}, bf16[256,64]{1,0:T(8,128)(2,1)}, u32[]{:S(2)}) copy-start(bf16[256,64]{1,0:T(8,128)(2,1)} %constant.14.clone.th) | copy-start | bytes 98308
  10.1 21.1 %copy-start.14 = (bf16[64,256]{1,0:T(8,128)(2,1)S(1)}, bf16[64,256]{1,0:T(8,128)(2,1)}, u32[]{:S(2)}) copy-start(bf16[64,256]{1,0:T(8,128)(2,1)} %constant.16.clone.lh.refs_3_) | copy-start | bytes 98308
  10.1 21.1 %copy-start.15 = (bf16[64,256]{1,0:T(8,128)(2,1)S(1)}, bf16[64,256]{1,0:T(8,128)(2,1)}, u32[]{:S(2)}) copy-start(bf16[64,256]{1,0:T(8,128)(2,1)} %constant.17.clone.ll.refs_4_) | copy-start | bytes 98308
  10.1 13.9 %all-to-all-start = ((s16[4,144,256]{2,1,0:T(8,128)(2,1)}), s16[4,144,256]{2,1,0:T(8,128)(2,1)S(1)}, u32[]{:S(2)}, u32[]{:S(2)}) async-start(s16[4,144,256]{2,1,0:T(8,128)(2,1)} %bitcast.17), calls=%async_computation | async-start | bytes 589824 | tf_op jit(solution)/shard_map/all_to_all | solution.py:364
  18.1 0.8 copy-start.17
  18.9 0.8 copy-start.18
  24.1 1.0 copy-start.1
  25.1 32.5 %all-to-all-start.1 = ((s16[4,528,256]{2,1,0:T(8,128)(2,1)}), s16[4,528,256]{2,1,0:T(8,128)(2,1)S(1)}, u32[]{:S(2)}, u32[]{:S(2)}) async-start(s16[4,528,256]{2,1,0:T(8,128)(2,1)} %bitcast.13), calls=%async_computation.1 | async-start | bytes 2162688 | tf_op jit(solution)/shard_map/all_to_all | solution.py:364
  31.3 1.2 %copy-start.2 = (f32[256,1024]{1,0:T(8,128)S(1)}, f32[256,1024]{1,0:T(8,128)}, u32[]{:S(2)}) copy-start(f32[256,1024]{1,0:T(8,128)} %momentum.3) | copy-start | bytes 3145732
  33.8 0.8 copy-start.4
  57.6 8.4 %copy-start.21 = (s32[8,128]{1,0:T(8,128)S(1)}, s32[8,128]{1,0:T(8,128)}, u32[]{:S(2)}) copy-start(s32[8,128]{1,0:T(8,128)} %copy-done.20) | copy-start | bytes 12292
  57.6 8.4 %collective-permute-start = (s16[2112,256]{1,0:T(8,128)(2,1)S(1)}, s16[2112,256]{1,0:T(8,128)(2,1)S(1)}, u32[]{:S(2)}, u32[]{:S(2)}) collective-permute-start(s16[2112,256]{1,0:T(8,128)(2,1)S(1)} %bitcast.11), channel_id=1, source_target_pairs={{0,1},{1,0},{2,3},{3,2},{4,5},{5,4},{6,7},{7,6},{8,9},{9,8},{10,11... | collective-permute-start | bytes 3244040 | tf_op jit(solution)/shard_map/ppermute | solution.py:390
  63.2 1.0 copy-start.5
  64.2 1.1 copy-start.8
  65.3 1.0 copy-start.6
  65.3 1.2 %copy-start.9 = (bf16[2,64,2048]{2,1,0:T(8,128)(2,1)S(1)}, bf16[2,64,2048]{2,1,0:T(8,128)(2,1)}, u32[]{:S(2)}) copy-start(bf16[2,64,2048]{2,1,0:T(8,128)(2,1)} %copy-done.7) | copy-start | bytes 1572868
  68.5 32.9 %all-to-all-start.2 = ((f32[512,1,128]{2,1,0:T(1,128)}), f32[512,1,128]{2,1,0:T(1,128)S(1)}, u32[]{:S(2)}, u32[]{:S(2)}) async-start(f32[512,1,128]{2,1,0:T(1,128)} %bitcast.8), calls=%async_computation.2 | async-start | bytes 524288 | tf_op jit(solution)/shard_map/all_to_all | solution.py:393
  84.5 1.2 %copy-start.3 = (f32[256,1024]{1,0:T(8,128)S(1)}, f32[256,1024]{1,0:T(8,128)}, u32[]{:S(2)}) copy-start(f32[256,1024]{1,0:T(8,128)} %momentum.3) | copy-start | bytes 3145732
  86.6 1.4 %copy-start.10 = (bf16[4,256,1024]{2,1,0:T(8,128)(2,1)}, bf16[4,256,1024]{2,1,0:T(8,128)(2,1)S(1)}, u32[]{:S(2)}) copy-start(bf16[4,256,1024]{2,1,0:T(8,128)(2,1)S(1)} %get-tuple-element.34.turned) | copy-start | bytes 6291460
  88.0 1.0 copy-start.11
  101.4 0.9 copy-start.22
  (4 other events, 2.7 us)
Sparse Core Ops, SparseCore 0:
  10.1 92.0 all-gather.1

commit v7 on v6

--- a/solution.py
+++ b/solution.py
@@ -74,7 +74,7 @@
         part = grads[:, q * 256:(q + 1) * 256]
         parts.append(dot(part, th[...]) + dot(part, tl[...]))
     band = jnp.concatenate(parts, axis=1)
-    top = jnp.maximum(jnp.max(jnp.abs(band), axis=1, keepdims=True), 1e-35)
+    top = jnp.maximum(jnp.max(jnp.abs(band), axis=1, keepdims=True), 1e-30)
     exponent = jnp.broadcast_to(jnp.ceil(jnp.log2(top)), (128, 128))
     code = jnp.floor(band * (power(-exponent[:, :1]) * LEVELS) + 0.5)
     scales = jnp.concatenate([exponent.T[:16]] * 2, axis=1)

time: 117 us -> 117 us (level)
  no operation moved by 1% of the time
where the time goes in v7:
time: 117 us; the launch traced here: 116 us
  waiting for transfers between devices  37.7 us (32%)
  starting transfers between devices  35.7 us (31%)
  Pallas kernels  14.7 us (13%)
  between operations  14.2 us (12%)
  local copies, waits for them, and re-layouts  13.6 us (12%)
    all_to_all x2, waiting for transfers between devices, exchange(): lax.all_to_all(copies, 'shard', 0, 0, tiled=True, axis_index_groups=groups)  23.8 us
    all_to_all x1, starting transfers between devices, body(): received = lax.all_to_all(board, ('rep', 'shard'), 0, 0, tiled=True)  16 us
    all_to_all x2, starting transfers between devices, exchange(): lax.all_to_all(copies, 'shard', 0, 0, tiled=True, axis_index_groups=groups)  14.1 us
    unnamed x46, local copies, waits for them, and re-layouts  13.6 us
    all_to_all x1, waiting for transfers between devices, body(): received = lax.all_to_all(board, ('rep', 'shard'), 0, 0, tiled=True)  12.4 us
    pallas_call x1, Pallas kernels, final(): pl.pallas_call(final_kernel, out_shape=(sds((ROWS, WIDTH)), sds((64, CH *...  6.88 us
    pallas_call x6, Pallas kernels, call(): pl.pallas_call(kernel, out_shape=shapes, in_specs=scalar + vmem(len(args)...  5.88 us
    ppermute x1, starting transfers between devices, body(): other = lax.ppermute(own, 'shard', OTHER_CORE)  5.56 us
  transfers between devices with their start and end apart: 5, of which 4 were waited for; matrix products, arithmetic and copies ran while one was open for 0% of the time, Pallas kernels for 7%

profile of v7, /device:TPU:1, one launch (start us, length us, event | category | flops | bytes accessed | tf_op | source)
XLA Modules:
  0.0 116.0 jit_solution(12014435359634940633)
XLA Ops:
  7.9 2.2 %project_kernel.1 = s16[576,256]{1,0:T(8,128)(2,1)} custom-call(bf16[128,1024]{1,0:T(8,128)(2,1)} %grads.1, bf16[256,64]{1,0:T(8,128)(2,1)} %constant.14.clone.th, bf16[256,64]{1,0:T(8,128)(2,1)} %constant.15.clone.tl), custom_call_target="tpu_custom_call" | custom-call | tf_op jit(solution)/shard_map/project_kernel/pallas_call | solution.py:310
  10.1 8.0 %all-to-all-start = ((s16[4,144,256]{2,1,0:T(8,128)(2,1)}), s16[4,144,256]{2,1,0:T(8,128)(2,1)S(1)}, u32[]{:S(2)}, u32[]{:S(2)}) async-start(s16[4,144,256]{2,1,0:T(8,128)(2,1)} %bitcast.17), calls=%async_computation | async-start | bytes 589824 | tf_op jit(solution)/shard_map/all_to_all | solution.py:364
  18.1 0.8 copy-done.17
  18.9 0.8 copy-done.18
  22.4 1.6 %all-to-all-done = s16[4,144,256]{2,1,0:T(8,128)(2,1)S(1)} async-done(((s16[4,144,256]{2,1,0:T(8,128)(2,1)}), s16[4,144,256]{2,1,0:T(8,128)(2,1)S(1)}, u32[]{:S(2)}, u32[]{:S(2)}) %all-to-all-start) | async-done | bytes 294944 | tf_op jit(solution)/shard_map/all_to_all | solution.py:364
  24.1 1.0 copy-done.1
  25.1 6.1 %all-to-all-start.1 = ((s16[4,528,256]{2,1,0:T(8,128)(2,1)}), s16[4,528,256]{2,1,0:T(8,128)(2,1)S(1)}, u32[]{:S(2)}, u32[]{:S(2)}) async-start(s16[4,528,256]{2,1,0:T(8,128)(2,1)} %bitcast.13), calls=%async_computation.1 | async-start | bytes 2162688 | tf_op jit(solution)/shard_map/all_to_all | solution.py:364
  31.3 1.2 %copy-done.2 = f32[256,1024]{1,0:T(8,128)S(1)} copy-done((f32[256,1024]{1,0:T(8,128)S(1)}, f32[256,1024]{1,0:T(8,128)}, u32[]{:S(2)}) %copy-start.2) | copy-done | bytes 1048600
  32.5 1.4 %prepare_kernel.1 = (bf16[2,64,2048]{2,1,0:T(8,128)(2,1)S(1)}, bf16[2,64,2048]{2,1,0:T(8,128)(2,1)S(1)}, f32[64,256]{1,0:T(8,128)S(1)}) custom-call(bf16[4096,256]{1,0:T(8,128)(2,1)S(1)} %copy-done, f32[256,1024]{1,0:T(8,128)S(1)} %copy-done.2, bf16[64,256]{1,0:T(8,128)(2,1)S(1)} %copy-done.14, bf16[64,256]{1,0:T(8,128)(2,1)S(1)} %copy-done.15, ...), custom_call_target="tpu_custom_call" | custom-call | tf_op jit(solution)/shard_map/prepare_kernel/pallas_call | solution.py:310
  33.8 0.8 copy-done.4
  34.6 0.8 copy-done.7
  35.4 22.2 %all-to-all-done.1 = s16[4,528,256]{2,1,0:T(8,128)(2,1)S(1)} async-done(((s16[4,528,256]{2,1,0:T(8,128)(2,1)}), s16[4,528,256]{2,1,0:T(8,128)(2,1)S(1)}, u32[]{:S(2)}, u32[]{:S(2)}) %all-to-all-start.1) | async-done | bytes 1081376 | tf_op jit(solution)/shard_map/all_to_all | solution.py:364
  57.6 5.6 %collective-permute-start = (s16[2112,256]{1,0:T(8,128)(2,1)S(1)}, s16[2112,256]{1,0:T(8,128)(2,1)S(1)}, u32[]{:S(2)}, u32[]{:S(2)}) collective-permute-start(s16[2112,256]{1,0:T(8,128)(2,1)S(1)} %bitcast.11), channel_id=1, source_target_pairs={{0,1},{1,0},{2,3},{3,2},{4,5},{5,4},{6,7},{7,6},{8,9},{9,8},{10,11... | collective-permute-start | bytes 3244040 | tf_op jit(solution)/shard_map/ppermute | solution.py:390
  63.2 1.0 copy-done.5
  64.2 1.1 copy-done.8
  66.5 2.0 %far.1 = (f32[64,256]{1,0:T(8,128)S(1)}, f32[512,128]{1,0:T(8,128)}) custom-call(s32[1]{0:T(128)} %bitcast.place, bf16[2,64,2048]{2,1,0:T(8,128)(2,1)S(1)} %copy-done.6, bf16[2,64,2048]{2,1,0:T(8,128)(2,1)S(1)} %copy-done.9, s16[2112,256]{1,0:T(8,128)(2,1)S(1)} %collective-permute-done.other, f32[64,256]{1,0:T(8,128)S(1)} %near_kernel.1.near, ...), custom_call_target="tpu_custom_call" | custom-call | tf_op jit(solution)/shard_map/far/pallas_call | solution.py:321
  68.5 16.0 %all-to-all-start.2 = ((f32[512,1,128]{2,1,0:T(1,128)}), f32[512,1,128]{2,1,0:T(1,128)S(1)}, u32[]{:S(2)}, u32[]{:S(2)}) async-start(f32[512,1,128]{2,1,0:T(1,128)} %bitcast.8), calls=%async_computation.2 | async-start | bytes 524288 | tf_op jit(solution)/shard_map/all_to_all | solution.py:393
  84.5 1.2 %copy-done.3 = f32[256,1024]{1,0:T(8,128)S(1)} copy-done((f32[256,1024]{1,0:T(8,128)S(1)}, f32[256,1024]{1,0:T(8,128)}, u32[]{:S(2)}) %copy-start.3) | copy-done | bytes 1048600
  85.7 0.9 ready_kernel.1
  86.6 1.4 %copy-done.10 = bf16[4,256,1024]{2,1,0:T(8,128)(2,1)} copy-done((bf16[4,256,1024]{2,1,0:T(8,128)(2,1)}, bf16[4,256,1024]{2,1,0:T(8,128)(2,1)S(1)}, u32[]{:S(2)}) %copy-start.10) | copy-done | bytes 2097176
  88.0 1.0 copy-done.11
  89.0 12.4 %all-to-all-done.2 = f32[512,1,128]{2,1,0:T(1,128)S(1)} async-done(((f32[512,1,128]{2,1,0:T(1,128)}), f32[512,1,128]{2,1,0:T(1,128)S(1)}, u32[]{:S(2)}, u32[]{:S(2)}) %all-to-all-start.2) | async-done | bytes 262176 | tf_op jit(solution)/shard_map/all_to_all | solution.py:393
  101.4 0.9 all-gather.2.cloned.1.call-done.grads
  102.2 6.9 %final.1 = (f32[256,1024]{1,0:T(8,128)}, bf16[64,4096]{1,0:T(8,128)(2,1)}) custom-call(bf16[4,256,1024]{2,1,0:T(8,128)(2,1)} %copy-done.10, bf16[4096,1024]{1,0:T(8,128)(2,1)} %all-gather.2.cloned.1.call-done.grads, f32[256,1024]{1,0:T(8,128)} %copy-done.11, f32[512,128]{1,0:T(8,128)} %bitcast.18, s32[64,256]{1,0:T(8,128)} %copy-done.16, ...), custom_call_target="tpu_custom_call" | custom-call | flops 2147483648 | bytes 14680064 | tf_op jit(solution)/shard_map/final/pallas_call | solution.py:335
  (41 shorter events, 4.7 us)
Async XLA Ops:
  7.2 95.1 %all-gather.2.cloned.1.call-start = ((), (), s32[]{:S(2)}) async-start(), calls=%async_computation.3 | async-start | bytes 8650752 | tf_op jit(solution)/shard_map/all_gather | solution.py:371
  10.1 21.1 %copy-start = (bf16[4096,256]{1,0:T(8,128)(2,1)S(1)}, bf16[4096,256]{1,0:T(8,128)(2,1)}, u32[]{:S(2)}) copy-start(bf16[4096,256]{1,0:T(8,128)(2,1)} %inputs.3) | copy-start | bytes 6291460
  10.1 21.1 %copy-start.12 = (bf16[256,64]{1,0:T(8,128)(2,1)S(1)}, bf16[256,64]{1,0:T(8,128)(2,1)}, u32[]{:S(2)}) copy-start(bf16[256,64]{1,0:T(8,128)(2,1)} %constant.15.clone.tl) | copy-start | bytes 98308
  10.1 21.1 %copy-start.13 = (bf16[256,64]{1,0:T(8,128)(2,1)S(1)}, bf16[256,64]{1,0:T(8,128)(2,1)}, u32[]{:S(2)}) copy-start(bf16[256,64]{1,0:T(8,128)(2,1)} %constant.14.clone.th) | copy-start | bytes 98308
  10.1 21.1 %copy-start.14 = (bf16[64,256]{1,0:T(8,128)(2,1)S(1)}, bf16[64,256]{1,0:T(8,128)(2,1)}, u32[]{:S(2)}) copy-start(bf16[64,256]{1,0:T(8,128)(2,1)} %constant.16.clone.lh.refs_3_) | copy-start | bytes 98308
  10.1 21.1 %copy-start.15 = (bf16[64,256]{1,0:T(8,128)(2,1)S(1)}, bf16[64,256]{1,0:T(8,128)(2,1)}, u32[]{:S(2)}) copy-start(bf16[64,256]{1,0:T(8,128)(2,1)} %constant.17.clone.ll.refs_4_) | copy-start | bytes 98308
  10.1 13.9 %all-to-all-start = ((s16[4,144,256]{2,1,0:T(8,128)(2,1)}), s16[4,144,256]{2,1,0:T(8,128)(2,1)S(1)}, u32[]{:S(2)}, u32[]{:S(2)}) async-start(s16[4,144,256]{2,1,0:T(8,128)(2,1)} %bitcast.17), calls=%async_computation | async-start | bytes 589824 | tf_op jit(solution)/shard_map/all_to_all | solution.py:364
  18.1 0.8 copy-start.17
  18.9 0.8 copy-start.18
  24.1 1.0 copy-start.1
  25.1 32.5 %all-to-all-start.1 = ((s16[4,528,256]{2,1,0:T(8,128)(2,1)}), s16[4,528,256]{2,1,0:T(8,128)(2,1)S(1)}, u32[]{:S(2)}, u32[]{:S(2)}) async-start(s16[4,528,256]{2,1,0:T(8,128)(2,1)} %bitcast.13), calls=%async_computation.1 | async-start | bytes 2162688 | tf_op jit(solution)/shard_map/all_to_all | solution.py:364
  31.3 1.2 %copy-start.2 = (f32[256,1024]{1,0:T(8,128)S(1)}, f32[256,1024]{1,0:T(8,128)}, u32[]{:S(2)}) copy-start(f32[256,1024]{1,0:T(8,128)} %momentum.3) | copy-start | bytes 3145732
  33.8 0.8 copy-start.4
  57.6 8.4 %copy-start.21 = (s32[8,128]{1,0:T(8,128)S(1)}, s32[8,128]{1,0:T(8,128)}, u32[]{:S(2)}) copy-start(s32[8,128]{1,0:T(8,128)} %copy-done.20) | copy-start | bytes 12292
  57.6 8.4 %collective-permute-start = (s16[2112,256]{1,0:T(8,128)(2,1)S(1)}, s16[2112,256]{1,0:T(8,128)(2,1)S(1)}, u32[]{:S(2)}, u32[]{:S(2)}) collective-permute-start(s16[2112,256]{1,0:T(8,128)(2,1)S(1)} %bitcast.11), channel_id=1, source_target_pairs={{0,1},{1,0},{2,3},{3,2},{4,5},{5,4},{6,7},{7,6},{8,9},{9,8},{10,11... | collective-permute-start | bytes 3244040 | tf_op jit(solution)/shard_map/ppermute | solution.py:390
  63.2 1.0 copy-start.5
  64.2 1.1 copy-start.8
  65.3 1.0 copy-start.6
  65.3 1.2 %copy-start.9 = (bf16[2,64,2048]{2,1,0:T(8,128)(2,1)S(1)}, bf16[2,64,2048]{2,1,0:T(8,128)(2,1)}, u32[]{:S(2)}) copy-start(bf16[2,64,2048]{2,1,0:T(8,128)(2,1)} %copy-done.7) | copy-start | bytes 1572868
  68.5 32.9 %all-to-all-start.2 = ((f32[512,1,128]{2,1,0:T(1,128)}), f32[512,1,128]{2,1,0:T(1,128)S(1)}, u32[]{:S(2)}, u32[]{:S(2)}) async-start(f32[512,1,128]{2,1,0:T(1,128)} %bitcast.8), calls=%async_computation.2 | async-start | bytes 524288 | tf_op jit(solution)/shard_map/all_to_all | solution.py:393
  84.5 1.2 %copy-start.3 = (f32[256,1024]{1,0:T(8,128)S(1)}, f32[256,1024]{1,0:T(8,128)}, u32[]{:S(2)}) copy-start(f32[256,1024]{1,0:T(8,128)} %momentum.3) | copy-start | bytes 3145732
  86.6 1.4 %copy-start.10 = (bf16[4,256,1024]{2,1,0:T(8,128)(2,1)}, bf16[4,256,1024]{2,1,0:T(8,128)(2,1)S(1)}, u32[]{:S(2)}) copy-start(bf16[4,256,1024]{2,1,0:T(8,128)(2,1)S(1)} %get-tuple-element.34.turned) | copy-start | bytes 6291460
  88.0 1.0 copy-start.11
  101.4 0.9 copy-start.22
  (4 other events, 2.7 us)
Sparse Core Ops, SparseCore 0:
  10.1 92.0 all-gather.1
